TPU v7x, 256 devices: a whole 4x4x8 slice. The times are simulated.
256 devices in a mesh: dp: 2 (over x_hi), tensor: 8 (over y, core), context: 16 (over x_lo, z).
Axes of the slice: x: 4 (x_hi: 2, x_lo: 2; x = x_hi * 2 + x_lo), y: 4, z: 8, core: 2. Of those that a mesh axis runs over, the one named last changes fastest.
Arguments:
- gate_out: bfloat16 [4096, 8192], P(('dp', 'context'), 'tensor'), parts along dimension 0, may hold values from -6 to 6
- gate_in: bfloat16 [4096, 8192], P(('dp', 'context'), 'tensor'), parts along dimension 0, may hold values from -6 to 6
- values_in: bfloat16 [4096, 8192], P(('dp', 'context'), 'tensor'), parts along dimension 0, may hold values from -6 to 6
- long_filter: bfloat16 [2048, 8192], P('context', 'tensor'), may hold values from -0.125 to 0.125
- skip_gain: float32 [8192], P('tensor'), may hold values from 0.25 to 2
- grad_out: bfloat16 [4096, 8192], P(('dp', 'context'), 'tensor'), parts along dimension 0, may hold values from -6 to 6
Outputs:
- grad_gate_out: bfloat16 [4096, 8192], P(('dp', 'context'), 'tensor'), parts along dimension 0
- grad_gate_in: bfloat16 [4096, 8192], P(('dp', 'context'), 'tensor'), parts along dimension 0
- grad_values: bfloat16 [4096, 8192], P(('dp', 'context'), 'tensor'), parts along dimension 0
- grad_filter: float32 [4096, 8192], P(('dp', 'context'), 'tensor'), parts along dimension 0
There are 2 independent parts, one for each index of `dp`. A program takes and returns all parts, laid end to end along the dimension named above; an argument that names none is the same for every part. Nothing has to cross between parts.
All inputs are finite; a program needn't handle non-finite values.
Results may differ from a plain program's by a relative error of at most 0.0013.
Values sent between devices are 32-bit elements; how exact they have to be, the bound alone decides.
No kernel may reach another device: no remote copies, remote signals or barrier semaphores. Data moves between devices by JAX's collectives and lax.ppermute only.
A program may use at most 64 MiB of HBM per device.

v0:
```python
import math

import jax
import jax.numpy as jnp
from jax import lax
from jax.sharding import PartitionSpec as P

COLS = 128


def angle_table(outer_idx, inner_idx, length):
    product = outer_idx[:, None] * inner_idx[None, :] % length
    return product.astype(jnp.float32) * (2.0 * math.pi / length)


def rows_forward(signal, length):
    inner_idx = jnp.arange(signal.shape[1], dtype=jnp.int32)
    outer_idx = jnp.arange(length, dtype=jnp.int32)
    angles = angle_table(outer_idx, inner_idx, length)
    real_part = jnp.einsum(
        "kn,bncd->bkcd", jnp.cos(angles), signal, precision=lax.Precision.HIGHEST
    )
    imag_part = -jnp.einsum(
        "kn,bncd->bkcd", jnp.sin(angles), signal, precision=lax.Precision.HIGHEST
    )
    return jnp.stack([real_part, imag_part], axis=1)


def twiddle(spectrum, row_idx, col_idx, length, sign_val):
    angles = angle_table(row_idx, col_idx, length)[:, :, None]
    cosine = jnp.cos(angles)
    sine_part = sign_val * jnp.sin(angles)
    real_part = spectrum[:, 0]
    imag_part = spectrum[:, 1]
    return jnp.stack(
        [real_part * cosine - imag_part * sine_part, imag_part * cosine + real_part * sine_part],
        axis=1,
    )


def contract(weights_tab, operand):
    return jnp.einsum("mn,bknd->bkmd", weights_tab, operand, precision=lax.Precision.HIGHEST)


def cols_transform(spectrum, sign_val):
    count_cols = spectrum.shape[3]
    col_idx = jnp.arange(count_cols, dtype=jnp.int32)
    angles = angle_table(col_idx, col_idx, count_cols)
    cosine = jnp.cos(angles)
    sine_part = sign_val * jnp.sin(angles)
    real_part = spectrum[:, 0]
    imag_part = spectrum[:, 1]
    new_real = contract(cosine, real_part) - contract(sine_part, imag_part)
    new_imag = contract(cosine, imag_part) + contract(sine_part, real_part)
    return jnp.stack([new_real, new_imag], axis=1)


def rows_inverse(spectrum, count_out, length):
    rows_all = spectrum.shape[2]
    angles = angle_table(
        jnp.arange(count_out, dtype=jnp.int32), jnp.arange(rows_all, dtype=jnp.int32), rows_all
    )
    real_out = jnp.einsum(
        "nk,bkcd->bncd", jnp.cos(angles), spectrum[:, 0], precision=lax.Precision.HIGHEST
    )
    real_out = real_out - jnp.einsum(
        "nk,bkcd->bncd", jnp.sin(angles), spectrum[:, 1], precision=lax.Precision.HIGHEST
    )
    return real_out * (1.0 / length)


def spectral_products(spectrum):
    mixed_re, mixed_im = (spectrum[0, 0], spectrum[0, 1])
    filt_re, filt_im = (spectrum[1, 0], spectrum[1, 1])
    grad_re, grad_im = (spectrum[2, 0], spectrum[2, 1])
    conv_spec = jnp.stack(
        [filt_re * mixed_re - filt_im * mixed_im, filt_re * mixed_im + filt_im * mixed_re]
    )
    back_spec = jnp.stack(
        [filt_re * grad_re + filt_im * grad_im, filt_re * grad_im - filt_im * grad_re]
    )
    lag_spec = jnp.stack(
        [mixed_re * grad_re + mixed_im * grad_im, mixed_re * grad_im - mixed_im * grad_re]
    )
    return jnp.stack([conv_spec, back_spec, lag_spec])


def local(gate_out, gate_in, values_in, long_filter, skip_gain, grad_out):
    tokens, channels = gate_out.shape
    devices = lax.axis_size("context")
    position = lax.axis_index("context")
    seq_len = tokens * devices
    length = 2 * seq_len
    rows_all = length // COLS
    mixed_in = gate_in.astype(jnp.float32) * values_in.astype(jnp.float32)
    grad_mixed = grad_out.astype(jnp.float32) * gate_out.astype(jnp.float32)
    stacked = jnp.stack([mixed_in, long_filter.astype(jnp.float32), grad_mixed])
    local_cols = COLS // devices
    local_rows = rows_all // devices
    blocks = stacked.reshape(3, tokens // COLS, COLS, channels)
    blocks = lax.all_to_all(blocks, "context", split_axis=2, concat_axis=1, tiled=True)
    spectrum = rows_forward(blocks, rows_all)
    col_idx = position * local_cols + jnp.arange(local_cols, dtype=jnp.int32)
    spectrum = twiddle(spectrum, jnp.arange(rows_all, dtype=jnp.int32), col_idx, length, -1.0)
    spectrum = lax.all_to_all(spectrum, "context", split_axis=2, concat_axis=3, tiled=True)
    spectrum = cols_transform(spectrum, -1.0)
    spectrum = spectral_products(spectrum)
    spectrum = cols_transform(spectrum, 1.0)
    row_idx = position * local_rows + jnp.arange(local_rows, dtype=jnp.int32)
    spectrum = twiddle(spectrum, row_idx, jnp.arange(COLS, dtype=jnp.int32), length, 1.0)
    spectrum = lax.all_to_all(spectrum, "context", split_axis=3, concat_axis=2, tiled=True)
    result = rows_inverse(spectrum, rows_all // 2, length)
    result = lax.all_to_all(result, "context", split_axis=1, concat_axis=2, tiled=True)
    result = result.reshape(3, tokens, channels)
    mixer_state = result[0] + skip_gain[None, :] * mixed_in
    grad_mix = result[1] + skip_gain[None, :] * grad_mixed
    grad_filter = result[2] * (1.0 / math.sqrt(seq_len))
    grad_gate_out = (grad_out.astype(jnp.float32) * mixer_state).astype(jnp.bfloat16)
    grad_gate_in = (grad_mix * values_in.astype(jnp.float32)).astype(jnp.bfloat16)
    grad_values = (grad_mix * gate_in.astype(jnp.float32)).astype(jnp.bfloat16)
    return (grad_gate_out, grad_gate_in, grad_values, grad_filter)


def solution(mesh):
    return jax.shard_map(
        local,
        mesh=mesh,
        in_specs=(
            P(("dp", "context"), "tensor"),
            P(("dp", "context"), "tensor"),
            P(("dp", "context"), "tensor"),
            P("context", "tensor"),
            P("tensor"),
            P(("dp", "context"), "tensor"),
        ),
        out_specs=(
            P(("dp", "context"), "tensor"),
            P(("dp", "context"), "tensor"),
            P(("dp", "context"), "tensor"),
            P(("dp", "context"), "tensor"),
        ),
        check_vma=False,
    )
```

profile of v0, /device:TPU:1, one launch (start us, length us, event | category | flops | bytes accessed | tf_op | source)
XLA Modules:
  0.0 487.8 jit_solution(2327576290838996777)
XLA Ops:
  0.6 1.0 bitcast_convert_fusion
  1.6 1.4 fusion.27
  3.1 2.8 copy.52
  5.9 10.3 %all-to-all-start = ((f32[3,1,128,1024]{3,1,0,2:T(1,128)}), f32[3,1,128,1024]{3,1,0,2:T(1,128)S(1)}, u32[]{:S(2)}, u32[]{:S(2)}) async-start(f32[3,1,128,1024]{3,1,0,2:T(1,128)} %copy.52), calls=%async_computation | async-start | bytes 3145728 | tf_op jit(solution)/shard_map/all_to_all | solution.py:101
  16.4 35.8 %all-to-all-done = f32[3,1,128,1024]{3,1,0,2:T(1,128)S(1)} async-done(((f32[3,1,128,1024]{3,1,0,2:T(1,128)}), f32[3,1,128,1024]{3,1,0,2:T(1,128)S(1)}, u32[]{:S(2)}, u32[]{:S(2)}) %all-to-all-start) | async-done | bytes 1572896 | tf_op jit(solution)/shard_map/all_to_all | solution.py:101
  52.5 4.3 fusion.16
  56.8 5.0 %fusion.3 = (f32[3,1,32,8,1024]{4,2,3,0,1:T(8,128)S(1)}, f32[3,1,32,8,1024]{4,2,3,0,1:T(8,128)S(1)}) fusion(f32[3,8,1024,32]{2,3,1,0:T(8,128)S(1)} %fusion.16, f32[32,8]{0,1:T(8,128)S(1)} %get-tuple-element.20, f32[32,8]{0,1:T(8,128)S(1)} %get-tuple-element.19, f32[3,16,8,1024]{3,2,1,0:T(8,128)S(1)} %bitcast.186), kind=kOutput, calls=%fused_computation.16 | convolution fusion | flops 156507136 | bytes 11012096 | tf_op jit(solution)/shard_map/kn,bncd->bkcd/dot_general | solution.py:20
  61.8 1.1 pad_maximum_fusion
  62.9 6.9 %copy.56 = f32[3,2,32,8,1024]{4,3,0,1,2:T(8,128)} copy(f32[3,2,32,8,1024]{4,2,3,0,1:T(8,128)S(1)} %pad_maximum_fusion) | data formatting | bytes 12582912 | tf_op jit(solution)/shard_map/stack | solution.py:35
  69.8 6.7 %all-to-all-start.1 = ((f32[3,2,32,8,1024]{4,3,0,1,2:T(8,128)}), f32[3,2,32,8,1024]{4,3,0,1,2:T(8,128)}, u32[]{:S(2)}, u32[]{:S(2)}) async-start(f32[3,2,32,8,1024]{4,3,0,1,2:T(8,128)} %copy.56), calls=%async_computation.1 | async-start | bytes 12582912 | tf_op jit(solution)/shard_map/all_to_all | solution.py:105
  76.6 139.5 %all-to-all-done.1 = f32[3,2,32,8,1024]{4,3,0,1,2:T(8,128)} async-done(((f32[3,2,32,8,1024]{4,3,0,1,2:T(8,128)}), f32[3,2,32,8,1024]{4,3,0,1,2:T(8,128)}, u32[]{:S(2)}, u32[]{:S(2)}) %all-to-all-start.1) | async-done | bytes 6291488 | tf_op jit(solution)/shard_map/all_to_all | solution.py:105
  216.1 3.4 copy.90
  219.5 5.2 %fusion.7 = f32[3,2,1024,128]{3,2,1,0:T(8,128)S(1)} fusion(f32[3,2,2,128,1024]{4,3,2,1,0:T(8,128)S(1)} %bitcast.180), kind=kOutput, calls=%fused_computation.26 | convolution fusion | flops 1208188928 | bytes 6291456 | tf_op jit(solution)/shard_map/mn,bknd->bkmd/dot_general | solution.py:42
  224.7 5.2 %fusion.6 = f32[3,2,1024,128]{3,2,1,0:T(8,128)S(1)} fusion(f32[3,2,2,128,1024]{4,3,2,1,0:T(8,128)S(1)} %bitcast.181), kind=kOutput, calls=%fused_computation.25 | convolution fusion | flops 1208205312 | bytes 6291456 | tf_op jit(solution)/shard_map/mn,bknd->bkmd/dot_general | solution.py:42
  229.9 5.5 %subtract_bitcast_fusion.1 = f32[3,2,128,1024]{2,3,1,0:T(8,128)S(1)} fusion(f32[3,2,1024,128]{3,2,1,0:T(8,128)S(1)} %fusion.7, f32[3,2,2,128,1024]{4,3,2,1,0:T(8,128)S(1)} %bitcast.182), kind=kOutput, calls=%fused_computation.24 | convolution fusion | flops 1208991744 | bytes 9437184 | tf_op jit(solution)/shard_map/mn,bknd->bkmd/dot_general | solution.py:42
  235.5 5.2 %add_bitcast_fusion.1 = f32[3,2,128,1024]{2,3,1,0:T(8,128)S(1)} fusion(f32[3,2,1024,128]{3,2,1,0:T(8,128)S(1)} %fusion.6, f32[3,2,2,128,1024]{4,3,2,1,0:T(8,128)S(1)} %bitcast.183), kind=kOutput, calls=%fused_computation.23 | convolution fusion | flops 1208975360 | bytes 9437184 | tf_op jit(solution)/shard_map/mn,bknd->bkmd/dot_general | solution.py:42
  242.5 3.2 fusion.11
  245.7 2.8 fusion.10
  248.6 3.0 fusion.14
  251.6 3.5 subtract_bitcast_fusion
  255.1 3.5 pad_maximum_fusion.2
  258.6 10.4 %copy.61 = f32[3,2,2,128,1024]{4,2,0,1,3:T(2,128)} copy(f32[3,2,2,128,1024]{3,4,2,0,1:T(8,128)} %pad_maximum_fusion.2) | data formatting | bytes 12582912 | tf_op jit(solution)/shard_map/stack | solution.py:35
  268.9 146.4 %all_to_all.57 = f32[3,2,2,128,1024]{4,2,0,1,3:T(2,128)S(1)} all-to-all(f32[3,2,2,128,1024]{4,2,0,1,3:T(2,128)} %copy.61), channel_id=1, replica_groups=mesh['dp'=2,'tensor'=8,'context'=16] {'context'}, dimensions={3} | all-to-all | bytes 12582912 | tf_op jit(solution)/shard_map/all_to_all | solution.py:111
  415.3 3.6 copy.91
  419.0 7.5 %copy.63 = f32[3,2,16,2,8,1024]{5,3,2,4,0,1:T(2,128)} copy(f32[3,2,16,2,8,1024]{5,4,2,3,1,0:T(8,128)S(1)} %bitcast.184) | data formatting | bytes 12582912 | tf_op jit(solution)/shard_map/all_to_all | solution.py:111
  426.5 8.6 %all_to_all.51 = f32[3,2,32,8,1024]{4,2,3,0,1:T(8,128)} reshape(f32[3,2,16,2,8,1024]{5,3,2,4,0,1:T(2,128)} %copy.63) | data formatting | bytes 12582912 | tf_op jit(solution)/shard_map/all_to_all | solution.py:111
  435.1 3.7 fusion
  438.9 3.9 multiply_bitcast_fusion
  442.9 0.9 copy.64
  443.8 41.7 %all_to_all.58 = f32[3,16,8,1024]{3,2,0,1:T(8,128)S(1)} all-to-all(f32[3,16,8,1024]{3,2,0,1:T(8,128)S(1)} %copy.64), channel_id=1, replica_groups=mesh['dp'=2,'tensor'=8,'context'=16] {'context'}, dimensions={1} | all-to-all | bytes 3145728 | tf_op jit(solution)/shard_map/all_to_all | solution.py:113
  485.5 0.8 fusion.24
  486.4 1.2 fusion.21
  (22 shorter events, 2.5 us)
Async XLA Ops:
  5.9 46.3 %all-to-all-start = ((f32[3,1,128,1024]{3,1,0,2:T(1,128)}), f32[3,1,128,1024]{3,1,0,2:T(1,128)S(1)}, u32[]{:S(2)}, u32[]{:S(2)}) async-start(f32[3,1,128,1024]{3,1,0,2:T(1,128)} %copy.52), calls=%async_computation | async-start | bytes 3145728 | tf_op jit(solution)/shard_map/all_to_all | solution.py:101
  69.8 146.3 %all-to-all-start.1 = ((f32[3,2,32,8,1024]{4,3,0,1,2:T(8,128)}), f32[3,2,32,8,1024]{4,3,0,1,2:T(8,128)}, u32[]{:S(2)}, u32[]{:S(2)}) async-start(f32[3,2,32,8,1024]{4,3,0,1,2:T(8,128)} %copy.56), calls=%async_computation.1 | async-start | bytes 12582912 | tf_op jit(solution)/shard_map/all_to_all | solution.py:105
  442.8 43.6 %copy-start = (bf16[128,1024]{1,0:T(8,128)(2,1)S(1)}, bf16[128,1024]{1,0:T(8,128)(2,1)}, u32[]{:S(2)}) copy-start(bf16[128,1024]{1,0:T(8,128)(2,1)} %param.7) | copy-start | bytes 786436
  442.8 43.6 %copy-start.1 = (bf16[128,1024]{1,0:T(8,128)(2,1)S(1)}, bf16[128,1024]{1,0:T(8,128)(2,1)}, u32[]{:S(2)}) copy-start(bf16[128,1024]{1,0:T(8,128)(2,1)} %param.6) | copy-start | bytes 786436
  442.8 43.5 %copy-start.2 = (bf16[128,1024]{1,0:T(8,128)(2,1)S(1)}, bf16[128,1024]{1,0:T(8,128)(2,1)}, u32[]{:S(2)}) copy-start(bf16[128,1024]{1,0:T(8,128)(2,1)} %param.11) | copy-start | bytes 786436
  442.8 43.5 %copy-start.3 = (bf16[128,1024]{1,0:T(8,128)(2,1)S(1)}, bf16[128,1024]{1,0:T(8,128)(2,1)}, u32[]{:S(2)}) copy-start(bf16[128,1024]{1,0:T(8,128)(2,1)} %param.8) | copy-start | bytes 786436
  442.8 43.5 %copy-start.4 = (f32[1024]{0:T(1024)S(1)}, f32[1024]{0:T(1024)}, u32[]{:S(2)}) copy-start(f32[1024]{0:T(1024)} %param.10) | copy-start | bytes 12292
where the time goes:
time: 493 us; the launch traced here: 488 us
  blocking collectives  188 us (38%)
  waiting for transfers between devices  175 us (35%)
  matrix products  50.6 us (10%)
  local copies, waits for them, and re-layouts  44.5 us (9%)
  starting transfers between devices  17 us (3%)
  other arithmetic  11.2 us (2%)
    all_to_all x1, blocking collectives, local(): lax.all_to_all(spectrum, 'context', split_axis=3, concat_axis=2, tiled=True)  146 us
    all_to_all x1, waiting for transfers between devices, local(): lax.all_to_all(spectrum, 'context', split_axis=2, concat_axis=3, tiled=True)  140 us
    all_to_all x1, blocking collectives, local(): lax.all_to_all(result, 'context', split_axis=1, concat_axis=2, tiled=True)  41.7 us
    all_to_all x1, waiting for transfers between devices, local(): lax.all_to_all(blocks, 'context', split_axis=2, concat_axis=1, tiled=True)  35.8 us
    dot_general x8, matrix products, contract(): jnp.einsum('mn,bknd->bkmd', weights_tab, operand, precision=lax.Precision...  33.7 us
    all_to_all x3, local copies, waits for them, and re-layouts, local(): lax.all_to_all(spectrum, 'context', split_axis=3, concat_axis=2, tiled=True)  19.8 us
    another operation x2, local copies, waits for them, and re-layouts, twiddle(): jnp.stack([real_part * cosine - imag_part * sine_part, imag_part * cosine...  17.2 us
    all_to_all x1, starting transfers between devices, local(): lax.all_to_all(blocks, 'context', split_axis=2, concat_axis=1, tiled=True)  10.3 us
  transfers between devices with their start and end apart: 2, of which 2 were waited for; matrix products, arithmetic and copies ran while one was open for 0% of the time, Pallas kernels for 0%

commit v1 on v0

v1 whole, which is shorter than its diff:
```python
import math

import jax
import jax.numpy as jnp
import numpy as np
from jax import lax
from jax.experimental import pallas as pl
from jax.experimental.pallas import tpu as pltpu
from jax.sharding import PartitionSpec as P

LANES = 128
SIGNALS = 3


def complex_add(a, b):
    return (a[0] + b[0], a[1] + b[1])


def complex_sub(a, b):
    return (a[0] - b[0], a[1] - b[1])


def rotate(a, angle_num, angle_den):
    num = angle_num % angle_den
    re, im = a
    if num == 0:
        return a
    if 4 * num == angle_den:
        return (-im, re)
    if 2 * num == angle_den:
        return (-re, -im)
    if 4 * num == 3 * angle_den:
        return (im, -re)
    if (8 * num) % angle_den == 0:
        half = math.sqrt(0.5)
        octant = (8 * num) // angle_den
        if octant == 1:
            return ((re - im) * half, (re + im) * half)
        if octant == 3:
            return ((re + im) * -half, (re - im) * half)
        if octant == 5:
            return ((im - re) * half, (re + im) * -half)
        return ((re + im) * half, (im - re) * half)
    c = math.cos(2.0 * math.pi * num / angle_den)
    s = math.sin(2.0 * math.pi * num / angle_den)
    return (re * c - im * s, re * s + im * c)


def complex_fft(values, sign):
    n = len(values)
    if n == 1:
        return values
    half = n // 2
    sums = [complex_add(values[p], values[p + half]) for p in range(half)]
    diffs = [complex_sub(values[p], values[p + half]) for p in range(half)]
    diffs = [rotate(d, sign * p, n) for p, d in enumerate(diffs)]
    even = complex_fft(sums, sign)
    odd = complex_fft(diffs, sign)
    return [v for pair in zip(even, odd) for v in pair]


def odd_forward(diffs, n, out):
    quarter = n // 4
    if n == 2:
        out[1] = (diffs[0], None)
        return
    twisted = [rotate((diffs[p], -diffs[p + quarter]), -p, n) for p in range(quarter)]
    for r, value in enumerate(complex_fft(twisted, -1)):
        k = 4 * r + 1
        if 2 * k < n:
            out[k] = value
        else:
            out[n - k] = (value[0], -value[1])


def real_forward(values, n):
    out = {}
    half = n // 2
    if len(values) == half:
        sums, diffs = values, values
    else:
        sums = [values[p] + values[p + half] for p in range(half)]
        diffs = [values[p] - values[p + half] for p in range(half)]
    if half == 1:
        out[0] = (sums[0], None)
    else:
        for k, value in real_forward(sums, half).items():
            out[2 * k] = value
    odd_forward(diffs, n, out)
    return out


def real_inverse(spec, n, first_half):
    half, quarter = n // 2, n // 4
    if n == 2:
        return [spec[0][0] + spec[1][0], spec[0][0] - spec[1][0]]
    evens = real_inverse({k // 2: v for k, v in spec.items() if k % 2 == 0}, half, False)
    odds = []
    for r in range(quarter):
        k = 4 * r + 1
        odds.append(spec[k] if 2 * k < n else (spec[n - k][0], -spec[n - k][1]))
    turned = [rotate(v, p, n) for p, v in enumerate(complex_fft(odds, 1))]
    odd_part = [v[0] for v in turned] + [-v[1] for v in turned]
    front = [evens[p] + odd_part[p] for p in range(half)]
    if first_half:
        return front
    return front + [evens[p] - odd_part[p] for p in range(half)]


def table(blocks):
    rows_all = 2 * blocks
    length = rows_all * LANES
    lane = np.arange(LANES)
    out = []
    for k1 in range(blocks + 1):
        angles = 2.0 * np.pi * (lane[:, None] * (k1 + rows_all * lane[None, :]) % length) / length
        cosine, sine = np.cos(angles), np.sin(angles)
        out.append(np.block([[cosine, -sine], [sine, cosine]]))
    whole = np.stack(out).astype(np.float32)
    high = whole.astype(jnp.bfloat16)
    low = (whole - high.astype(np.float32)).astype(jnp.bfloat16)
    return high, low


def split(value):
    high = value.astype(jnp.bfloat16)
    return high, (value - high.astype(jnp.float32)).astype(jnp.bfloat16)


def dot_parts(left, right_high, right_low, right_dim):
    dims = (((1,), (right_dim,)), ((), ()))
    high, low = split(left)
    total = lax.dot_general(low, right_high, dims, preferred_element_type=jnp.float32)
    total += lax.dot_general(high, right_low, dims, preferred_element_type=jnp.float32)
    return total + lax.dot_general(high, right_high, dims, preferred_element_type=jnp.float32)


def pack_kernel(gate_in, values_in, long_filter, grad_out, gate_out, packed):
    share = packed.shape[1] // SIGNALS
    mixed = gate_in[...].astype(jnp.float32) * values_in[...].astype(jnp.float32)
    grad = grad_out[...].astype(jnp.float32) * gate_out[...].astype(jnp.float32)
    for s, value in enumerate((mixed, long_filter[...].astype(jnp.float32), grad)):
        turned = value.T
        for b in range(packed.shape[0]):
            packed[b, s * share:(s + 1) * share, :] = turned[b * share:(b + 1) * share]


def convolve_kernel(received, high, low, result, spectrum, inverted):
    blocks, rows, _ = received.shape
    share = rows // SIGNALS
    rows_all = 2 * blocks
    scale = 2.0 / (rows_all * LANES)

    def forward(tile, carry):
        at = pl.ds(pl.multiple_of(tile * 8, 8), 8)
        out = real_forward([received[p, at, :] for p in range(blocks)], rows_all)
        for k1 in range(blocks + 1):
            re, im = out[k1]
            spectrum[k1, at, :LANES] = re
            spectrum[k1, at, LANES:] = jnp.zeros_like(re) if im is None else im
        return carry

    lax.fori_loop(0, rows // 8, forward, 0)

    for k1 in range(blocks + 1):
        freq = dot_parts(spectrum[k1], high[k1], low[k1], 0)
        mixed_re, mixed_im = freq[:share, :LANES], freq[:share, LANES:]
        filt_re, filt_im = freq[share:2 * share, :LANES], freq[share:2 * share, LANES:]
        grad_re, grad_im = freq[2 * share:, :LANES], freq[2 * share:, LANES:]
        factor = scale * 0.5 if k1 in (0, blocks) else scale
        grad_re, grad_im = grad_re * factor, grad_im * factor
        filt_scaled_re, filt_scaled_im = filt_re * factor, filt_im * factor
        conv = jnp.concatenate([
            filt_scaled_re * mixed_re - filt_scaled_im * mixed_im,
            filt_scaled_re * mixed_im + filt_scaled_im * mixed_re], axis=1)
        back = jnp.concatenate([
            filt_re * grad_re + filt_im * grad_im, filt_re * grad_im - filt_im * grad_re], axis=1)
        lag = jnp.concatenate([
            mixed_re * grad_re + mixed_im * grad_im, mixed_re * grad_im - mixed_im * grad_re], axis=1)
        products = jnp.concatenate([conv, back, lag], axis=0)
        inverted[k1] = dot_parts(products, high[k1], low[k1], 1)

    def backward(tile, carry):
        at = pl.ds(pl.multiple_of(tile * 8, 8), 8)
        spec = {k1: (inverted[k1, at, :LANES], inverted[k1, at, LANES:]) for k1 in range(blocks + 1)}
        for p, value in enumerate(real_inverse(spec, rows_all, True)):
            result[p, at, :] = value
        return carry

    lax.fori_loop(0, rows // 8, backward, 0)


def unpack_kernel(seq_len, returned, gate_in, values_in, skip_gain, grad_out, gate_out,
                  grad_gate_out, grad_gate_in, grad_values, grad_filter):
    share = returned.shape[1] // SIGNALS
    values, gate = values_in[...].astype(jnp.float32), gate_in[...].astype(jnp.float32)
    cotangent = grad_out[...].astype(jnp.float32)
    skip = skip_gain[...]

    def turned(s):
        return jnp.concatenate(
            [returned[b, s * share:(s + 1) * share, :] for b in range(returned.shape[0])], axis=0).T

    mixer_state = turned(0) + skip * (gate * values)
    grad_gate_out[...] = (cotangent * mixer_state).astype(jnp.bfloat16)
    grad_mix = turned(1) + skip * (cotangent * gate_out[...].astype(jnp.float32))
    grad_gate_in[...] = (grad_mix * values).astype(jnp.bfloat16)
    grad_values[...] = (grad_mix * gate).astype(jnp.bfloat16)
    grad_filter[...] = turned(2) * (1.0 / math.sqrt(seq_len))


def local(gate_out, gate_in, values_in, long_filter, skip_gain, grad_out):
    tokens, channels = gate_out.shape
    devices = lax.axis_size("context")
    seq_len = tokens * devices
    share = channels // devices
    rows = SIGNALS * share
    group = LANES // share
    steps = channels // LANES
    high, low = table(devices)

    def plain(columns_dim=1):
        return pl.BlockSpec((tokens, LANES), lambda i: (0, i))

    packed_spec = pl.BlockSpec((group, rows, tokens), lambda i: (i, 0, 0))
    packed = pl.pallas_call(
        pack_kernel,
        grid=(steps,),
        in_specs=[plain()] * 5,
        out_specs=packed_spec,
        out_shape=jax.ShapeDtypeStruct((devices, rows, tokens), jnp.float32),
        name="pack",
    )(gate_in, values_in, long_filter, grad_out, gate_out)
    received = lax.all_to_all(packed, "context", split_axis=0, concat_axis=0, tiled=True)
    result = pl.pallas_call(
        convolve_kernel,
        out_shape=jax.ShapeDtypeStruct((devices, rows, tokens), jnp.float32),
        in_specs=[pl.BlockSpec(memory_space=pltpu.VMEM)] * 3,
        out_specs=pl.BlockSpec(memory_space=pltpu.VMEM),
        scratch_shapes=[pltpu.VMEM((devices + 1, rows, 2 * LANES), jnp.float32)] * 2,
        compiler_params=pltpu.CompilerParams(vmem_limit_bytes=40 * 1024 * 1024),
        name="convolve",
    )(received, jnp.asarray(high), jnp.asarray(low))
    returned = lax.all_to_all(result, "context", split_axis=0, concat_axis=0, tiled=True)
    wide = [jax.ShapeDtypeStruct((tokens, channels), jnp.bfloat16)] * 3
    return tuple(pl.pallas_call(
        lambda *refs: unpack_kernel(seq_len, *refs),
        grid=(steps,),
        in_specs=[packed_spec, plain(), plain(), pl.BlockSpec((1, LANES), lambda i: (0, i)), plain(), plain()],
        out_specs=[plain()] * 4,
        out_shape=wide + [jax.ShapeDtypeStruct((tokens, channels), jnp.float32)],
        name="unpack",
    )(returned, gate_in, values_in, skip_gain[None, :], grad_out, gate_out))


def solution(mesh):
    sequence = P(("dp", "context"), "tensor")
    return jax.shard_map(
        local,
        mesh=mesh,
        in_specs=(sequence, sequence, sequence, P("context", "tensor"), P("tensor"), sequence),
        out_specs=(sequence,) * 4,
        check_vma=False,
    )
```

time: 493 us -> 108 us (0.22)
  the two profiles are of different devices: /device:TPU:1 before, /device:TPU:46 now
where the time goes in v1:
time: 108 us
  blocking collectives  89.5 us (83%)
  Pallas kernels  17.4 us (16%)
    all_to_all x1, blocking collectives, local(): lax.all_to_all(packed, 'context', split_axis=0, concat_axis=0, tiled=True)  47.2 us
    all_to_all x1, blocking collectives, local(): lax.all_to_all(result, 'context', split_axis=0, concat_axis=0, tiled=True)  42.3 us
    pallas_call x1, Pallas kernels, local(): pl.pallas_call(convolve_kernel, out_shape=jax.ShapeDtypeStruct((devices,...  5.94 us
    pallas_call x1, Pallas kernels, local(): pl.pallas_call(lambda *refs: unpack_kernel(seq_len, *refs), grid=(steps,)...  5.87 us
    pallas_call x1, Pallas kernels, local(): pl.pallas_call(pack_kernel, grid=(steps,), in_specs=[plain()] * 5, out_sp...  5.6 us

profile of v1, /device:TPU:46, one launch (start us, length us, event | category | flops | bytes accessed | tf_op | source)
XLA Modules:
  0.0 107.6 jit_solution(17839965170009231951)
XLA Ops:
  0.6 0.0 copy-start.1
  0.6 5.6 %pack.1 = f32[16,192,128]{2,1,0:T(8,128)} custom-call(bf16[128,1024]{1,0:T(8,128)(2,1)} %refs_1_.1, bf16[128,1024]{1,0:T(8,128)(2,1)} %refs_2_.1, bf16[128,1024]{1,0:T(8,128)(2,1)} %long_filter.1, bf16[128,1024]{1,0:T(8,128)(2,1)} %refs_4_.1, bf16[128,1024]{1,0:T(8,128)(2,1)} %refs_5_.1), custom_call_target="tpu_custom_call" | custom-call | tf_op jit(solution)/shard_map/pack/pallas_call | solution.py:226
  6.2 0.0 copy-start
  6.2 47.2 %all_to_all.10.received = f32[16,192,128]{2,1,0:T(8,128)S(1)} all-to-all(f32[16,192,128]{2,1,0:T(8,128)} %pack.1), channel_id=1, replica_groups=mesh['dp'=2,'tensor'=8,'context'=16] {'context'}, dimensions={0} | all-to-all | bytes 3145728 | tf_op jit(solution)/shard_map/all_to_all | solution.py:234
  53.5 0.0 copy-done.1
  53.5 0.0 copy-done
  53.5 5.9 %convolve.1 = f32[16,192,128]{2,1,0:T(8,128)S(1)} custom-call(f32[16,192,128]{2,1,0:T(8,128)S(1)} %all_to_all.10.received, bf16[17,256,256]{2,1,0:T(8,128)(2,1)S(1)} %copy-done.1, bf16[17,256,256]{2,1,0:T(8,128)(2,1)S(1)} %copy-done), custom_call_target="tpu_custom_call" | custom-call | tf_op jit(solution)/shard_map/convolve/pallas_call | solution.py:235
  59.4 42.3 %all_to_all.11.refs_0_ = f32[16,192,128]{2,1,0:T(8,128)} all-to-all(f32[16,192,128]{2,1,0:T(8,128)S(1)} %convolve.1), channel_id=1, replica_groups=mesh['dp'=2,'tensor'=8,'context'=16] {'context'}, dimensions={0} | all-to-all | bytes 3145728 | tf_op jit(solution)/shard_map/all_to_all | solution.py:244
  101.7 5.9 %unpack.1 = (bf16[128,1024]{1,0:T(8,128)(2,1)}, bf16[128,1024]{1,0:T(8,128)(2,1)}, bf16[128,1024]{1,0:T(8,128)(2,1)}, f32[128,1024]{1,0:T(8,128)}) custom-call(f32[16,192,128]{2,1,0:T(8,128)} %all_to_all.11.refs_0_, bf16[128,1024]{1,0:T(8,128)(2,1)} %refs_1_.1, bf16[128,1024]{1,0:T(8,128)(2,1)} %refs_2_.1, f32[1,1024]{1,0:T(1,128)} %bitcast.1, ...), custom_call_target="tpu_custom_call" | custom-call | tf_op jit(solution)/shard_map/unpack/pallas_call | solution.py:246
Async XLA Ops:
  0.6 52.8 %copy-start.1 = (bf16[17,256,256]{2,1,0:T(8,128)(2,1)S(1)}, bf16[17,256,256]{2,1,0:T(8,128)(2,1)}, u32[]{:S(2)}) copy-start(bf16[17,256,256]{2,1,0:T(8,128)(2,1)} %constant.4.clone.high) | copy-start | bytes 6684676
  6.2 47.2 %copy-start = (bf16[17,256,256]{2,1,0:T(8,128)(2,1)S(1)}, bf16[17,256,256]{2,1,0:T(8,128)(2,1)}, u32[]{:S(2)}) copy-start(bf16[17,256,256]{2,1,0:T(8,128)(2,1)} %constant.5.clone.low) | copy-start | bytes 6684676

commit v2 on v1

v2 whole, which is shorter than its diff:
```python
import math

import jax
import jax.numpy as jnp
import numpy as np
from jax import lax
from jax.experimental import pallas as pl
from jax.experimental.pallas import tpu as pltpu
from jax.sharding import PartitionSpec as P

LANES = 128
AXES = ("line", "dp", "column")


def complex_add(a, b):
    return (a[0] + b[0], a[1] + b[1])


def complex_sub(a, b):
    return (a[0] - b[0], a[1] - b[1])


def rotate(a, angle_num, angle_den):
    num = angle_num % angle_den
    re, im = a
    if num == 0:
        return a
    if 4 * num == angle_den:
        return (-im, re)
    if 2 * num == angle_den:
        return (-re, -im)
    if 4 * num == 3 * angle_den:
        return (im, -re)
    if (8 * num) % angle_den == 0:
        half = math.sqrt(0.5)
        octant = (8 * num) // angle_den
        if octant == 1:
            return ((re - im) * half, (re + im) * half)
        if octant == 3:
            return ((re + im) * -half, (re - im) * half)
        if octant == 5:
            return ((im - re) * half, (re + im) * -half)
        return ((re + im) * half, (im - re) * half)
    c = math.cos(2.0 * math.pi * num / angle_den)
    s = math.sin(2.0 * math.pi * num / angle_den)
    return (re * c - im * s, re * s + im * c)


def complex_fft(values, sign):
    n = len(values)
    if n == 1:
        return values
    half = n // 2
    sums = [complex_add(values[p], values[p + half]) for p in range(half)]
    diffs = [complex_sub(values[p], values[p + half]) for p in range(half)]
    diffs = [rotate(d, sign * p, n) for p, d in enumerate(diffs)]
    even = complex_fft(sums, sign)
    odd = complex_fft(diffs, sign)
    return [v for pair in zip(even, odd) for v in pair]


def odd_forward(diffs, n, out):
    quarter = n // 4
    if n == 2:
        out[1] = (diffs[0], None)
        return
    twisted = [rotate((diffs[p], -diffs[p + quarter]), -p, n) for p in range(quarter)]
    for r, value in enumerate(complex_fft(twisted, -1)):
        k = 4 * r + 1
        if 2 * k < n:
            out[k] = value
        else:
            out[n - k] = (value[0], -value[1])


def real_forward(values, n):
    out = {}
    half = n // 2
    if len(values) == half:
        sums, diffs = values, values
    else:
        sums = [values[p] + values[p + half] for p in range(half)]
        diffs = [values[p] - values[p + half] for p in range(half)]
    if half == 1:
        out[0] = (sums[0], None)
    else:
        for k, value in real_forward(sums, half).items():
            out[2 * k] = value
    odd_forward(diffs, n, out)
    return out


def real_inverse(spec, n, first_half):
    half, quarter = n // 2, n // 4
    if n == 2:
        return [spec[0][0] + spec[1][0], spec[0][0] - spec[1][0]]
    evens = real_inverse({k // 2: v for k, v in spec.items() if k % 2 == 0}, half, False)
    odds = []
    for r in range(quarter):
        k = 4 * r + 1
        odds.append(spec[k] if 2 * k < n else (spec[n - k][0], -spec[n - k][1]))
    turned = [rotate(v, p, n) for p, v in enumerate(complex_fft(odds, 1))]
    odd_part = [v[0] for v in turned] + [-v[1] for v in turned]
    front = [evens[p] + odd_part[p] for p in range(half)]
    if first_half:
        return front
    return front + [evens[p] - odd_part[p] for p in range(half)]


def table(blocks):
    rows_all = 2 * blocks
    length = rows_all * LANES
    lane = np.arange(LANES)
    out = []
    for k1 in range(blocks + 1):
        angles = 2.0 * np.pi * (lane[:, None] * (k1 + rows_all * lane[None, :]) % length) / length
        cosine, sine = np.cos(angles), np.sin(angles)
        out.append(np.block([[cosine, -sine], [sine, cosine]]))
    whole = np.stack(out).astype(np.float32)
    high = whole.astype(jnp.bfloat16)
    low = (whole - high.astype(np.float32)).astype(jnp.bfloat16)
    return high, low


def split(value):
    high = value.astype(jnp.bfloat16)
    return high, (value - high.astype(jnp.float32)).astype(jnp.bfloat16)


def dot_parts(left, right_high, right_low, right_dim):
    dims = (((1,), (right_dim,)), ((), ()))
    high, low = split(left)
    total = lax.dot_general(low, right_high, dims, preferred_element_type=jnp.float32)
    total += lax.dot_general(high, right_low, dims, preferred_element_type=jnp.float32)
    return total + lax.dot_general(high, right_high, dims, preferred_element_type=jnp.float32)


def pack_kernel(gate_in, values_in, long_filter, grad_out, gate_out, packed):
    share = channels_of(packed.shape[1], 1 + 1 + 0.5)
    mixed = gate_in[...].astype(jnp.float32) * values_in[...].astype(jnp.float32)
    grad = grad_out[...].astype(jnp.float32) * gate_out[...].astype(jnp.float32)
    filt = long_filter[...].astype(jnp.float32)
    half = share // 2
    second = lax.axis_index("dp") == 1
    for lane in range(0, mixed.shape[1], LANES):
        at = slice(lane, lane + LANES)
        mixed_t, grad_t, filt_t = mixed[:, at].T, grad[:, at].T, filt[:, at].T
        for b in range(LANES // share):
            to, row = lane // share + b, b * share
            packed[to, :share, :] = mixed_t[row:row + share]
            packed[to, share:2 * share, :] = grad_t[row:row + share]
            packed[to, 2 * share:, :] = jnp.where(
                second, filt_t[row + half:row + share], filt_t[row:row + half])


def channels_of(rows, signals):
    return int(rows / signals)


def convolve_kernel(shape, received, high, low, result, spectrum, inverted):
    lines, parts, columns = shape
    blocks = lines * columns
    share = result.shape[1] // 3
    half = share // 2
    rows_all = 2 * blocks
    scale = 2.0 / (rows_all * LANES)
    grad_row, filt_row = parts * share, 2 * parts * share

    def source(line, part, column):
        return (line * parts + part) * columns + column

    def forward(part, taken, given):
        out = real_forward(
            [received[source(x, part, z), pl.ds(taken, 8), :] for x in range(lines) for z in range(columns)],
            rows_all)
        for k1 in range(blocks + 1):
            re, im = out[k1]
            spectrum[k1, pl.ds(given, 8), :LANES] = re
            spectrum[k1, pl.ds(given, 8), LANES:] = jnp.zeros_like(re) if im is None else im

    for part in range(parts):
        def tile_of_signals(tile, carry):
            start = pl.multiple_of(tile * 8, 8)
            forward(part, start, pl.multiple_of(part * share + start, 8))
            forward(part, pl.multiple_of(share + start, 8), pl.multiple_of(grad_row + part * share + start, 8))
            return carry

        lax.fori_loop(0, share // 8, tile_of_signals, 0)

        def tile_of_filter(tile, carry):
            start = pl.multiple_of(tile * 8, 8)
            forward(part, pl.multiple_of(2 * share + start, 8), pl.multiple_of(filt_row + part * half + start, 8))
            return carry

        lax.fori_loop(0, half // 8, tile_of_filter, 0)

    for k1 in range(blocks + 1):
        freq = dot_parts(spectrum[k1], high[k1], low[k1], 0)
        factor = scale * 0.5 if k1 in (0, blocks) else scale
        filt_re, filt_im = freq[filt_row:, :LANES], freq[filt_row:, LANES:]
        filt_re, filt_im = filt_re * factor, filt_im * factor
        products = []
        for part in range(parts):
            mixed = slice(part * share, (part + 1) * share)
            grad = slice(grad_row + part * share, grad_row + (part + 1) * share)
            mixed_re, mixed_im = freq[mixed, :LANES], freq[mixed, LANES:]
            grad_re, grad_im = freq[grad, :LANES], freq[grad, LANES:]
            products.append(jnp.concatenate([
                filt_re * mixed_re - filt_im * mixed_im, filt_re * mixed_im + filt_im * mixed_re], axis=1))
            products.append(jnp.concatenate([
                filt_re * grad_re + filt_im * grad_im, filt_re * grad_im - filt_im * grad_re], axis=1))
            mixed_re, mixed_im = mixed_re * factor, mixed_im * factor
            products.append(jnp.concatenate([
                mixed_re * grad_re + mixed_im * grad_im, mixed_re * grad_im - mixed_im * grad_re], axis=1))
        inverted[k1] = dot_parts(jnp.concatenate(products, axis=0), high[k1], low[k1], 1)

    for part in range(parts):
        def backward(tile, carry):
            start = pl.multiple_of(tile * 8, 8)
            at = pl.ds(pl.multiple_of(part * 3 * share + start, 8), 8)
            spec = {k1: (inverted[k1, at, :LANES], inverted[k1, at, LANES:]) for k1 in range(blocks + 1)}
            values = real_inverse(spec, rows_all, True)
            for x in range(lines):
                for z in range(columns):
                    result[source(x, part, z), pl.ds(start, 8), :] = values[x * columns + z]
            return carry

        lax.fori_loop(0, 3 * share // 8, backward, 0)


def unpack_kernel(seq_len, returned, gate_in, values_in, skip_gain, grad_out, gate_out,
                  grad_gate_out, grad_gate_in, grad_values, grad_filter):
    share = returned.shape[1] // 3
    for lane in range(0, gate_in.shape[1], LANES):
        at = slice(lane, lane + LANES)
        values, gate = values_in[:, at].astype(jnp.float32), gate_in[:, at].astype(jnp.float32)
        cotangent = grad_out[:, at].astype(jnp.float32)
        skip = skip_gain[:, at]

        def turned(s):
            return jnp.concatenate(
                [returned[lane // share + b, s * share:(s + 1) * share, :] for b in range(LANES // share)],
                axis=0).T

        mixer_state = turned(0) + skip * (gate * values)
        grad_gate_out[:, at] = (cotangent * mixer_state).astype(jnp.bfloat16)
        grad_mix = turned(1) + skip * (cotangent * gate_out[:, at].astype(jnp.float32))
        grad_gate_in[:, at] = (grad_mix * values).astype(jnp.bfloat16)
        grad_values[:, at] = (grad_mix * gate).astype(jnp.bfloat16)
        grad_filter[:, at] = turned(2) * (1.0 / math.sqrt(seq_len))


def pack(width, devices, gate_in, values_in, long_filter, grad_out, gate_out):
    tokens, channels = gate_in.shape
    share = channels // devices
    rows = 2 * share + share // 2
    plain = pl.BlockSpec((tokens, width), lambda i: (0, i))
    return pl.pallas_call(
        pack_kernel,
        grid=(channels // width,),
        in_specs=[plain] * 5,
        out_specs=pl.BlockSpec((width // share, rows, tokens), lambda i: (i, 0, 0)),
        out_shape=jax.ShapeDtypeStruct((devices, rows, tokens), jnp.float32),
        name="pack",
    )(gate_in, values_in, long_filter, grad_out, gate_out)


def convolve(shape, received, high, low):
    devices, rows, tokens = received.shape
    share = channels_of(rows, 2.5)
    blocks = shape[0] * shape[2]
    forward_rows = (2 * shape[1] + 1) * share
    inverse_rows = 3 * shape[1] * share
    return pl.pallas_call(
        lambda *refs: convolve_kernel(shape, *refs),
        out_shape=jax.ShapeDtypeStruct((devices, 3 * share, tokens), jnp.float32),
        in_specs=[pl.BlockSpec(memory_space=pltpu.VMEM)] * 3,
        out_specs=pl.BlockSpec(memory_space=pltpu.VMEM),
        scratch_shapes=[pltpu.VMEM((blocks + 1, forward_rows, 2 * LANES), jnp.float32),
                        pltpu.VMEM((blocks + 1, inverse_rows, 2 * LANES), jnp.float32)],
        compiler_params=pltpu.CompilerParams(vmem_limit_bytes=40 * 1024 * 1024),
        name="convolve",
    )(received, high, low)


def unpack(width, seq_len, returned, gate_in, values_in, skip_gain, grad_out, gate_out):
    devices, rows, tokens = returned.shape
    channels = gate_in.shape[1]
    share = channels // devices
    plain = pl.BlockSpec((tokens, width), lambda i: (0, i))
    wide = [jax.ShapeDtypeStruct((tokens, channels), jnp.bfloat16)] * 3
    return tuple(pl.pallas_call(
        lambda *refs: unpack_kernel(seq_len, *refs),
        grid=(channels // width,),
        in_specs=[pl.BlockSpec((width // share, rows, tokens), lambda i: (i, 0, 0)), plain, plain,
                  pl.BlockSpec((1, width), lambda i: (0, i)), plain, plain],
        out_specs=[plain] * 4,
        out_shape=wide + [jax.ShapeDtypeStruct((tokens, channels), jnp.float32)],
        name="unpack",
    )(returned, gate_in, values_in, skip_gain[None, :], grad_out, gate_out))


PACK_WIDTH = 256
UNPACK_WIDTH = 256


def local(gate_out, gate_in, values_in, long_filter, skip_gain, grad_out):
    tokens = gate_out.shape[0]
    shape = tuple(lax.axis_size(axis) for axis in AXES)
    blocks = shape[0] * shape[2]
    high, low = (jnp.asarray(t) for t in table(blocks))
    packed = pack(PACK_WIDTH, math.prod(shape), gate_in, values_in, long_filter, grad_out, gate_out)
    received = lax.all_to_all(packed, AXES, split_axis=0, concat_axis=0, tiled=True)
    result = convolve(shape, received, high, low)
    returned = lax.all_to_all(result, AXES, split_axis=0, concat_axis=0, tiled=True)
    return unpack(UNPACK_WIDTH, tokens * blocks, returned, gate_in, values_in, skip_gain, grad_out, gate_out)


def solution(mesh):
    parts, tensor, context = mesh.devices.shape
    lines = 2
    mesh = jax.sharding.Mesh(
        mesh.devices.reshape(parts, tensor, lines, context // lines), ("dp", "tensor", "line", "column"))
    sequence = P(("dp", "line", "column"), "tensor")
    return jax.shard_map(
        local,
        mesh=mesh,
        in_specs=(sequence, sequence, sequence, P(("line", "column"), "tensor"), P("tensor"), sequence),
        out_specs=(sequence,) * 4,
        check_vma=False,
    )
```

time: 108 us -> 105 us (0.972)
  the two profiles are of different devices: /device:TPU:46 before, /device:TPU:56 now
where the time goes in v2:
time: 105 us
  blocking collectives  90.3 us (86%)
  Pallas kernels  13.7 us (13%)
    all_to_all x1, blocking collectives, local(): lax.all_to_all(packed, AXES, split_axis=0, concat_axis=0, tiled=True)  46.2 us
    all_to_all x1, blocking collectives, local(): lax.all_to_all(result, AXES, split_axis=0, concat_axis=0, tiled=True)  44.1 us
    pallas_call x1, Pallas kernels, convolve(): pl.pallas_call(lambda *refs: convolve_kernel(shape, *refs), out_shape=jax...  5.89 us
    pallas_call x1, Pallas kernels, pack(): pl.pallas_call(pack_kernel, grid=(channels // width,), in_specs=[plain] *...  3.94 us
    pallas_call x1, Pallas kernels, unpack(): pl.pallas_call(lambda *refs: unpack_kernel(seq_len, *refs), grid=(channel...  3.89 us

profile of v2, /device:TPU:56, one launch (start us, length us, event | category | flops | bytes accessed | tf_op | source)
XLA Modules:
  0.0 104.7 jit_solution(17378031536880767829)
XLA Ops:
  0.6 0.0 copy-start.1
  0.6 3.9 %pack.1 = f32[32,80,128]{2,1,0:T(8,128)} custom-call(bf16[128,1024]{1,0:T(8,128)(2,1)} %refs_1_.2, bf16[128,1024]{1,0:T(8,128)(2,1)} %refs_2_.2, bf16[128,1024]{1,0:T(8,128)(2,1)} %long_filter.1, bf16[128,1024]{1,0:T(8,128)(2,1)} %refs_4_.1, bf16[128,1024]{1,0:T(8,128)(2,1)} %refs_5_.1), custom_call_target="tpu_custom_call" | custom-call | tf_op jit(solution)/shard_map/pack/pallas_call | solution.py:258
  4.6 0.0 copy-start
  4.6 46.2 %all_to_all.10.refs_0_ = f32[32,80,128]{2,1,0:T(8,128)S(1)} all-to-all(f32[32,80,128]{2,1,0:T(8,128)} %pack.1), channel_id=1, replica_groups=mesh['dp'=2,'tensor'=8,'line'=2,'column'=8] {'line','dp','column'}, dimensions={0} | all-to-all | bytes 2621440 | tf_op jit(solution)/shard_map/all_to_all | solution.py:313
  50.8 0.0 copy-done.1
  50.8 0.0 copy-done
  50.8 5.9 %convolve.1 = f32[32,96,128]{2,1,0:T(8,128)S(1)} custom-call(f32[32,80,128]{2,1,0:T(8,128)S(1)} %all_to_all.10.refs_0_, bf16[17,256,256]{2,1,0:T(8,128)(2,1)S(1)} %copy-done.1, bf16[17,256,256]{2,1,0:T(8,128)(2,1)S(1)} %copy-done), custom_call_target="tpu_custom_call" | custom-call | tf_op jit(solution)/shard_map/convolve/pallas_call | solution.py:274
  56.7 44.1 %all_to_all.11.refs_0_ = f32[32,96,128]{2,1,0:T(8,128)} all-to-all(f32[32,96,128]{2,1,0:T(8,128)S(1)} %convolve.1), channel_id=1, replica_groups=mesh['dp'=2,'tensor'=8,'line'=2,'column'=8] {'line','dp','column'}, dimensions={0} | all-to-all | bytes 3145728 | tf_op jit(solution)/shard_map/all_to_all | solution.py:315
  100.8 3.9 %unpack.1 = (bf16[128,1024]{1,0:T(8,128)(2,1)}, bf16[128,1024]{1,0:T(8,128)(2,1)}, bf16[128,1024]{1,0:T(8,128)(2,1)}, f32[128,1024]{1,0:T(8,128)}) custom-call(f32[32,96,128]{2,1,0:T(8,128)} %all_to_all.11.refs_0_, bf16[128,1024]{1,0:T(8,128)(2,1)} %refs_1_.2, bf16[128,1024]{1,0:T(8,128)(2,1)} %refs_2_.2, f32[1,1024]{1,0:T(1,128)} %bitcast.1, ...), custom_call_target="tpu_custom_call" | custom-call | tf_op jit(solution)/shard_map/unpack/pallas_call | solution.py:292
Async XLA Ops:
  0.6 50.2 %copy-start.1 = (bf16[17,256,256]{2,1,0:T(8,128)(2,1)S(1)}, bf16[17,256,256]{2,1,0:T(8,128)(2,1)}, u32[]{:S(2)}) copy-start(bf16[17,256,256]{2,1,0:T(8,128)(2,1)} %constant.4.clone.refs_1_) | copy-start | bytes 6684676
  4.6 46.2 %copy-start = (bf16[17,256,256]{2,1,0:T(8,128)(2,1)S(1)}, bf16[17,256,256]{2,1,0:T(8,128)(2,1)}, u32[]{:S(2)}) copy-start(bf16[17,256,256]{2,1,0:T(8,128)(2,1)} %constant.5.clone.refs_2_) | copy-start | bytes 6684676

commit v3 on v1

--- a/solution.py
+++ b/solution.py
@@ -9,7 +9,6 @@
 from jax.sharding import PartitionSpec as P
 
 LANES = 128
-SIGNALS = 3
 
 
 def complex_add(a, b):
@@ -135,19 +134,23 @@
     return total + lax.dot_general(high, right_high, dims, preferred_element_type=jnp.float32)
 
 
-def pack_kernel(gate_in, values_in, long_filter, grad_out, gate_out, packed):
-    share = packed.shape[1] // SIGNALS
+def pack_kernel(share, gate_in, values_in, long_filter, grad_out, gate_out, packed):
     mixed = gate_in[...].astype(jnp.float32) * values_in[...].astype(jnp.float32)
     grad = grad_out[...].astype(jnp.float32) * gate_out[...].astype(jnp.float32)
-    for s, value in enumerate((mixed, long_filter[...].astype(jnp.float32), grad)):
-        turned = value.T
-        for b in range(packed.shape[0]):
-            packed[b, s * share:(s + 1) * share, :] = turned[b * share:(b + 1) * share]
+    filt = long_filter[...].astype(jnp.float32)
+    for lane in range(0, mixed.shape[1], LANES):
+        at = slice(lane, lane + LANES)
+        mixed_t, grad_t, filt_t = mixed[:, at].T, grad[:, at].T, filt[:, at].T
+        for b in range(LANES // share):
+            to, row = lane // share + b, b * share
+            packed[to, :share, :] = mixed_t[row:row + share]
+            packed[to, share:2 * share, :] = filt_t[row:row + share]
+            packed[to, 2 * share:, :] = grad_t[row:row + share]
 
 
 def convolve_kernel(received, high, low, result, spectrum, inverted):
     blocks, rows, _ = received.shape
-    share = rows // SIGNALS
+    share = rows // 3
     rows_all = 2 * blocks
     scale = 2.0 / (rows_all * LANES)
 
@@ -192,65 +195,84 @@
 
 def unpack_kernel(seq_len, returned, gate_in, values_in, skip_gain, grad_out, gate_out,
                   grad_gate_out, grad_gate_in, grad_values, grad_filter):
-    share = returned.shape[1] // SIGNALS
-    values, gate = values_in[...].astype(jnp.float32), gate_in[...].astype(jnp.float32)
-    cotangent = grad_out[...].astype(jnp.float32)
-    skip = skip_gain[...]
-
-    def turned(s):
-        return jnp.concatenate(
-            [returned[b, s * share:(s + 1) * share, :] for b in range(returned.shape[0])], axis=0).T
-
-    mixer_state = turned(0) + skip * (gate * values)
-    grad_gate_out[...] = (cotangent * mixer_state).astype(jnp.bfloat16)
-    grad_mix = turned(1) + skip * (cotangent * gate_out[...].astype(jnp.float32))
-    grad_gate_in[...] = (grad_mix * values).astype(jnp.bfloat16)
-    grad_values[...] = (grad_mix * gate).astype(jnp.bfloat16)
-    grad_filter[...] = turned(2) * (1.0 / math.sqrt(seq_len))
-
-
-def local(gate_out, gate_in, values_in, long_filter, skip_gain, grad_out):
-    tokens, channels = gate_out.shape
-    devices = lax.axis_size("context")
-    seq_len = tokens * devices
+    share = returned.shape[1] // 3
+    for lane in range(0, gate_in.shape[1], LANES):
+        at = slice(lane, lane + LANES)
+        values, gate = values_in[:, at].astype(jnp.float32), gate_in[:, at].astype(jnp.float32)
+        cotangent = grad_out[:, at].astype(jnp.float32)
+        skip = skip_gain[:, at]
+
+        def turned(s):
+            return jnp.concatenate(
+                [returned[lane // share + b, s * share:(s + 1) * share, :] for b in range(LANES // share)],
+                axis=0).T
+
+        mixer_state = turned(0) + skip * (gate * values)
+        grad_gate_out[:, at] = (cotangent * mixer_state).astype(jnp.bfloat16)
+        grad_mix = turned(1) + skip * (cotangent * gate_out[:, at].astype(jnp.float32))
+        grad_gate_in[:, at] = (grad_mix * values).astype(jnp.bfloat16)
+        grad_values[:, at] = (grad_mix * gate).astype(jnp.bfloat16)
+        grad_filter[:, at] = turned(2) * (1.0 / math.sqrt(seq_len))
+
+
+def pack(width, devices, gate_in, values_in, long_filter, grad_out, gate_out):
+    tokens, channels = gate_in.shape
     share = channels // devices
-    rows = SIGNALS * share
-    group = LANES // share
-    steps = channels // LANES
-    high, low = table(devices)
-
-    def plain(columns_dim=1):
-        return pl.BlockSpec((tokens, LANES), lambda i: (0, i))
-
-    packed_spec = pl.BlockSpec((group, rows, tokens), lambda i: (i, 0, 0))
-    packed = pl.pallas_call(
-        pack_kernel,
-        grid=(steps,),
-        in_specs=[plain()] * 5,
-        out_specs=packed_spec,
+    rows = 3 * share
+    plain = pl.BlockSpec((tokens, width), lambda i: (0, i))
+    return pl.pallas_call(
+        lambda *refs: pack_kernel(share, *refs),
+        grid=(channels // width,),
+        in_specs=[plain] * 5,
+        out_specs=pl.BlockSpec((width // share, rows, tokens), lambda i: (i, 0, 0)),
         out_shape=jax.ShapeDtypeStruct((devices, rows, tokens), jnp.float32),
         name="pack",
     )(gate_in, values_in, long_filter, grad_out, gate_out)
-    received = lax.all_to_all(packed, "context", split_axis=0, concat_axis=0, tiled=True)
-    result = pl.pallas_call(
+
+
+def convolve(received, high, low):
+    blocks, rows, _ = received.shape
+    return pl.pallas_call(
         convolve_kernel,
-        out_shape=jax.ShapeDtypeStruct((devices, rows, tokens), jnp.float32),
+        out_shape=jax.ShapeDtypeStruct(received.shape, jnp.float32),
         in_specs=[pl.BlockSpec(memory_space=pltpu.VMEM)] * 3,
         out_specs=pl.BlockSpec(memory_space=pltpu.VMEM),
-        scratch_shapes=[pltpu.VMEM((devices + 1, rows, 2 * LANES), jnp.float32)] * 2,
+        scratch_shapes=[pltpu.VMEM((blocks + 1, rows, 2 * LANES), jnp.float32)] * 2,
         compiler_params=pltpu.CompilerParams(vmem_limit_bytes=40 * 1024 * 1024),
         name="convolve",
-    )(received, jnp.asarray(high), jnp.asarray(low))
-    returned = lax.all_to_all(result, "context", split_axis=0, concat_axis=0, tiled=True)
+    )(received, high, low)
+
+
+def unpack(width, seq_len, returned, gate_in, values_in, skip_gain, grad_out, gate_out):
+    devices, rows, tokens = returned.shape
+    channels = gate_in.shape[1]
+    share = channels // devices
+    plain = pl.BlockSpec((tokens, width), lambda i: (0, i))
     wide = [jax.ShapeDtypeStruct((tokens, channels), jnp.bfloat16)] * 3
     return tuple(pl.pallas_call(
         lambda *refs: unpack_kernel(seq_len, *refs),
-        grid=(steps,),
-        in_specs=[packed_spec, plain(), plain(), pl.BlockSpec((1, LANES), lambda i: (0, i)), plain(), plain()],
-        out_specs=[plain()] * 4,
+        grid=(channels // width,),
+        in_specs=[pl.BlockSpec((width // share, rows, tokens), lambda i: (i, 0, 0)), plain, plain,
+                  pl.BlockSpec((1, width), lambda i: (0, i)), plain, plain],
+        out_specs=[plain] * 4,
         out_shape=wide + [jax.ShapeDtypeStruct((tokens, channels), jnp.float32)],
         name="unpack",
     )(returned, gate_in, values_in, skip_gain[None, :], grad_out, gate_out))
+
+
+PACK_WIDTH = 512
+UNPACK_WIDTH = 512
+
+
+def local(gate_out, gate_in, values_in, long_filter, skip_gain, grad_out):
+    tokens = gate_out.shape[0]
+    blocks = lax.axis_size("context")
+    high, low = (jnp.asarray(t) for t in table(blocks))
+    packed = pack(PACK_WIDTH, blocks, gate_in, values_in, long_filter, grad_out, gate_out)
+    received = lax.all_to_all(packed, "context", split_axis=0, concat_axis=0, tiled=True)
+    result = convolve(received, high, low)
+    returned = lax.all_to_all(result, "context", split_axis=0, concat_axis=0, tiled=True)
+    return unpack(UNPACK_WIDTH, tokens * blocks, returned, gate_in, values_in, skip_gain, grad_out, gate_out)
 
 
 def solution(mesh):

time: 108 us -> 102 us (0.944)
  the two profiles are of different devices: /device:TPU:46 before, /device:TPU:42 now
where the time goes in v3:
time: 102 us
  blocking collectives  89.5 us (88%)
  Pallas kernels  11.5 us (11%)
    all_to_all x1, blocking collectives, local(): lax.all_to_all(packed, 'context', split_axis=0, concat_axis=0, tiled=True)  47.2 us
    all_to_all x1, blocking collectives, local(): lax.all_to_all(result, 'context', split_axis=0, concat_axis=0, tiled=True)  42.3 us
    pallas_call x1, Pallas kernels, convolve(): pl.pallas_call(convolve_kernel, out_shape=jax.ShapeDtypeStruct(received.s...  5.95 us
    pallas_call x1, Pallas kernels, unpack(): pl.pallas_call(lambda *refs: unpack_kernel(seq_len, *refs), grid=(channel...  2.81 us
    pallas_call x1, Pallas kernels, pack(): pl.pallas_call(lambda *refs: pack_kernel(share, *refs), grid=(channels //...  2.73 us

profile of v3, /device:TPU:42, one launch (start us, length us, event | category | flops | bytes accessed | tf_op | source)
XLA Modules:
  0.0 101.7 jit_solution(1769647433367345111)
XLA Ops:
  0.6 0.0 copy-start.1
  0.6 2.7 %pack.1 = f32[16,192,128]{2,1,0:T(8,128)} custom-call(bf16[128,1024]{1,0:T(8,128)(2,1)} %refs_1_.3, bf16[128,1024]{1,0:T(8,128)(2,1)} %refs_2_.3, bf16[128,1024]{1,0:T(8,128)(2,1)} %refs_2_.2, bf16[128,1024]{1,0:T(8,128)(2,1)} %refs_4_.3, bf16[128,1024]{1,0:T(8,128)(2,1)} %refs_5_.1), custom_call_target="tpu_custom_call" | custom-call | tf_op jit(solution)/shard_map/pack/pallas_call | solution.py:223
  3.4 0.0 copy-start
  3.4 47.2 %all_to_all.10.received = f32[16,192,128]{2,1,0:T(8,128)S(1)} all-to-all(f32[16,192,128]{2,1,0:T(8,128)} %pack.1), channel_id=1, replica_groups=mesh['dp'=2,'tensor'=8,'context'=16] {'context'}, dimensions={0} | all-to-all | bytes 3145728 | tf_op jit(solution)/shard_map/all_to_all | solution.py:272
  50.6 0.0 copy-done.1
  50.6 0.0 copy-done
  50.6 5.9 %convolve.1 = f32[16,192,128]{2,1,0:T(8,128)S(1)} custom-call(f32[16,192,128]{2,1,0:T(8,128)S(1)} %all_to_all.10.received, bf16[17,256,256]{2,1,0:T(8,128)(2,1)S(1)} %copy-done.1, bf16[17,256,256]{2,1,0:T(8,128)(2,1)S(1)} %copy-done), custom_call_target="tpu_custom_call" | custom-call | tf_op jit(solution)/shard_map/convolve/pallas_call | solution.py:235
  56.5 42.3 %all_to_all.11.refs_0_ = f32[16,192,128]{2,1,0:T(8,128)} all-to-all(f32[16,192,128]{2,1,0:T(8,128)S(1)} %convolve.1), channel_id=1, replica_groups=mesh['dp'=2,'tensor'=8,'context'=16] {'context'}, dimensions={0} | all-to-all | bytes 3145728 | tf_op jit(solution)/shard_map/all_to_all | solution.py:274
  98.9 2.8 %unpack.1 = (bf16[128,1024]{1,0:T(8,128)(2,1)}, bf16[128,1024]{1,0:T(8,128)(2,1)}, bf16[128,1024]{1,0:T(8,128)(2,1)}, f32[128,1024]{1,0:T(8,128)}) custom-call(f32[16,192,128]{2,1,0:T(8,128)} %all_to_all.11.refs_0_, bf16[128,1024]{1,0:T(8,128)(2,1)} %refs_1_.3, bf16[128,1024]{1,0:T(8,128)(2,1)} %refs_2_.3, f32[1,1024]{1,0:T(1,128)} %bitcast.1, ...), custom_call_target="tpu_custom_call" | custom-call | tf_op jit(solution)/shard_map/unpack/pallas_call | solution.py:252
Async XLA Ops:
  0.6 50.0 %copy-start.1 = (bf16[17,256,256]{2,1,0:T(8,128)(2,1)S(1)}, bf16[17,256,256]{2,1,0:T(8,128)(2,1)}, u32[]{:S(2)}) copy-start(bf16[17,256,256]{2,1,0:T(8,128)(2,1)} %constant.4.clone.high) | copy-start | bytes 6684676
  3.4 47.2 %copy-start = (bf16[17,256,256]{2,1,0:T(8,128)(2,1)S(1)}, bf16[17,256,256]{2,1,0:T(8,128)(2,1)}, u32[]{:S(2)}) copy-start(bf16[17,256,256]{2,1,0:T(8,128)(2,1)} %constant.5.clone.low) | copy-start | bytes 6684676

commit v4 on v2

--- a/solution.py
+++ b/solution.py
@@ -135,64 +135,64 @@
     return total + lax.dot_general(high, right_high, dims, preferred_element_type=jnp.float32)
 
 
-def pack_kernel(gate_in, values_in, long_filter, grad_out, gate_out, packed):
-    share = channels_of(packed.shape[1], 1 + 1 + 0.5)
+def rows_of(signal, share, parts):
+    return share // parts if signal == FILTER else share
+
+
+def pack_kernel(share, parts, plan, gate_in, values_in, long_filter, grad_out, gate_out, *packed):
     mixed = gate_in[...].astype(jnp.float32) * values_in[...].astype(jnp.float32)
     grad = grad_out[...].astype(jnp.float32) * gate_out[...].astype(jnp.float32)
-    filt = long_filter[...].astype(jnp.float32)
-    half = share // 2
-    second = lax.axis_index("dp") == 1
-    for lane in range(0, mixed.shape[1], LANES):
-        at = slice(lane, lane + LANES)
-        mixed_t, grad_t, filt_t = mixed[:, at].T, grad[:, at].T, filt[:, at].T
-        for b in range(LANES // share):
-            to, row = lane // share + b, b * share
-            packed[to, :share, :] = mixed_t[row:row + share]
-            packed[to, share:2 * share, :] = grad_t[row:row + share]
-            packed[to, 2 * share:, :] = jnp.where(
-                second, filt_t[row + half:row + share], filt_t[row:row + half])
-
-
-def channels_of(rows, signals):
-    return int(rows / signals)
-
-
-def convolve_kernel(shape, received, high, low, result, spectrum, inverted):
+    signals = {MIXED: mixed, FILTER: long_filter[...].astype(jnp.float32), GRAD: grad}
+    part = lax.axis_index("dp")
+    for out, members in zip(packed, plan):
+        given = 0
+        for signal in members:
+            count = rows_of(signal, share, parts)
+            for lane in range(0, mixed.shape[1], LANES):
+                turned = signals[signal][:, lane:lane + LANES].T
+                for b in range(LANES // share):
+                    kept = turned[b * share:b * share + count]
+                    for other in range(1, share // count):
+                        start = b * share + other * count
+                        kept = jnp.where(part == other, turned[start:start + count], kept)
+                    out[lane // share + b, given:given + count, :] = kept
+            given += count
+
+
+def convolve_kernel(shape, plan, *refs):
+    received, (high, low, result, spectrum, inverted) = refs[:len(plan)], refs[len(plan):]
     lines, parts, columns = shape
     blocks = lines * columns
     share = result.shape[1] // 3
-    half = share // 2
     rows_all = 2 * blocks
     scale = 2.0 / (rows_all * LANES)
     grad_row, filt_row = parts * share, 2 * parts * share
+    first_row = {MIXED: 0, GRAD: grad_row, FILTER: filt_row}
 
     def source(line, part, column):
         return (line * parts + part) * columns + column
 
-    def forward(part, taken, given):
-        out = real_forward(
-            [received[source(x, part, z), pl.ds(taken, 8), :] for x in range(lines) for z in range(columns)],
-            rows_all)
-        for k1 in range(blocks + 1):
-            re, im = out[k1]
-            spectrum[k1, pl.ds(given, 8), :LANES] = re
-            spectrum[k1, pl.ds(given, 8), LANES:] = jnp.zeros_like(re) if im is None else im
-
-    for part in range(parts):
-        def tile_of_signals(tile, carry):
-            start = pl.multiple_of(tile * 8, 8)
-            forward(part, start, pl.multiple_of(part * share + start, 8))
-            forward(part, pl.multiple_of(share + start, 8), pl.multiple_of(grad_row + part * share + start, 8))
-            return carry
-
-        lax.fori_loop(0, share // 8, tile_of_signals, 0)
-
-        def tile_of_filter(tile, carry):
-            start = pl.multiple_of(tile * 8, 8)
-            forward(part, pl.multiple_of(2 * share + start, 8), pl.multiple_of(filt_row + part * half + start, 8))
-            return carry
-
-        lax.fori_loop(0, half // 8, tile_of_filter, 0)
+    for operand, members in zip(received, plan):
+        taken_row = 0
+        for signal in members:
+            count = rows_of(signal, share, parts)
+            for part in range(parts):
+                given_row = first_row[signal] + part * count
+
+                def forward(tile, carry):
+                    taken = pl.ds(pl.multiple_of(taken_row + tile * 8, 8), 8)
+                    given = pl.ds(pl.multiple_of(given_row + tile * 8, 8), 8)
+                    out = real_forward(
+                        [operand[source(x, part, z), taken, :] for x in range(lines) for z in range(columns)],
+                        rows_all)
+                    for k1 in range(blocks + 1):
+                        re, im = out[k1]
+                        spectrum[k1, given, :LANES] = re
+                        spectrum[k1, given, LANES:] = jnp.zeros_like(re) if im is None else im
+                    return carry
+
+                lax.fori_loop(0, count // 8, forward, 0)
+            taken_row += count
 
     for k1 in range(blocks + 1):
         freq = dot_parts(spectrum[k1], high[k1], low[k1], 0)
@@ -250,37 +250,36 @@
         grad_filter[:, at] = turned(2) * (1.0 / math.sqrt(seq_len))
 
 
-def pack(width, devices, gate_in, values_in, long_filter, grad_out, gate_out):
+def pack(width, devices, parts, plan, gate_in, values_in, long_filter, grad_out, gate_out):
     tokens, channels = gate_in.shape
     share = channels // devices
-    rows = 2 * share + share // 2
+    rows = [sum(rows_of(signal, share, parts) for signal in members) for members in plan]
     plain = pl.BlockSpec((tokens, width), lambda i: (0, i))
     return pl.pallas_call(
-        pack_kernel,
+        lambda *refs: pack_kernel(share, parts, plan, *refs),
         grid=(channels // width,),
         in_specs=[plain] * 5,
-        out_specs=pl.BlockSpec((width // share, rows, tokens), lambda i: (i, 0, 0)),
-        out_shape=jax.ShapeDtypeStruct((devices, rows, tokens), jnp.float32),
+        out_specs=[pl.BlockSpec((width // share, r, tokens), lambda i: (i, 0, 0)) for r in rows],
+        out_shape=[jax.ShapeDtypeStruct((devices, r, tokens), jnp.float32) for r in rows],
         name="pack",
     )(gate_in, values_in, long_filter, grad_out, gate_out)
 
 
-def convolve(shape, received, high, low):
-    devices, rows, tokens = received.shape
-    share = channels_of(rows, 2.5)
+def convolve(shape, share, plan, received, high, low):
+    devices, _, tokens = received[0].shape
     blocks = shape[0] * shape[2]
     forward_rows = (2 * shape[1] + 1) * share
     inverse_rows = 3 * shape[1] * share
     return pl.pallas_call(
-        lambda *refs: convolve_kernel(shape, *refs),
+        lambda *refs: convolve_kernel(shape, plan, *refs),
         out_shape=jax.ShapeDtypeStruct((devices, 3 * share, tokens), jnp.float32),
-        in_specs=[pl.BlockSpec(memory_space=pltpu.VMEM)] * 3,
+        in_specs=[pl.BlockSpec(memory_space=pltpu.VMEM)] * (len(plan) + 2),
         out_specs=pl.BlockSpec(memory_space=pltpu.VMEM),
         scratch_shapes=[pltpu.VMEM((blocks + 1, forward_rows, 2 * LANES), jnp.float32),
                         pltpu.VMEM((blocks + 1, inverse_rows, 2 * LANES), jnp.float32)],
         compiler_params=pltpu.CompilerParams(vmem_limit_bytes=40 * 1024 * 1024),
         name="convolve",
-    )(received, high, low)
+    )(*received, high, low)
 
 
 def unpack(width, seq_len, returned, gate_in, values_in, skip_gain, grad_out, gate_out):
@@ -300,19 +299,36 @@
     )(returned, gate_in, values_in, skip_gain[None, :], grad_out, gate_out))
 
 
-PACK_WIDTH = 256
-UNPACK_WIDTH = 256
+PACK_WIDTH = 512
+UNPACK_WIDTH = 512
+MIXED, FILTER, GRAD = 0, 1, 2
+WHOLE = ((MIXED, FILTER, GRAD),)
+FILTER_FIRST = ((FILTER,), (MIXED, GRAD))
 
 
 def local(gate_out, gate_in, values_in, long_filter, skip_gain, grad_out):
-    tokens = gate_out.shape[0]
+    tokens, channels = gate_out.shape
     shape = tuple(lax.axis_size(axis) for axis in AXES)
+    devices = math.prod(shape)
     blocks = shape[0] * shape[2]
     high, low = (jnp.asarray(t) for t in table(blocks))
-    packed = pack(PACK_WIDTH, math.prod(shape), gate_in, values_in, long_filter, grad_out, gate_out)
-    received = lax.all_to_all(packed, AXES, split_axis=0, concat_axis=0, tiled=True)
-    result = convolve(shape, received, high, low)
-    returned = lax.all_to_all(result, AXES, split_axis=0, concat_axis=0, tiled=True)
+
+    def exchange(operand):
+        return lax.all_to_all(operand, AXES, split_axis=0, concat_axis=0, tiled=True)
+
+    def there_and_back(plan):
+        def run(*operands):
+            packed = pack(PACK_WIDTH, devices, shape[1], plan, *operands)
+            received = [exchange(packed[0])]
+            for part in packed[1:]:
+                part, _ = lax.optimization_barrier((part, received[-1][0, 0, 0]))
+                received.append(exchange(part))
+            return exchange(convolve(shape, channels // devices, plan, received, high, low))
+        return run
+
+    returned = lax.cond(
+        lax.axis_index("tensor") % 2 == 0, there_and_back(WHOLE), there_and_back(FILTER_FIRST),
+        gate_in, values_in, long_filter, grad_out, gate_out)
     return unpack(UNPACK_WIDTH, tokens * blocks, returned, gate_in, values_in, skip_gain, grad_out, gate_out)
 
 

time: 105 us -> 94.1 us (0.90)
  the two profiles are of different devices: /device:TPU:56 before, /device:TPU:1 now
where the time goes in v4:
time: 94.1 us; the launch traced here: 93.7 us
  blocking collectives  58.4 us (62%)
  Pallas kernels  12.6 us (13%)
  starting transfers between devices  12 us (13%)
  waiting for transfers between devices  10 us (11%)
    all_to_all x2, blocking collectives, exchange(): lax.all_to_all(operand, AXES, split_axis=0, concat_axis=0, tiled=True)  58.4 us
    all_to_all x1, starting transfers between devices, exchange(): lax.all_to_all(operand, AXES, split_axis=0, concat_axis=0, tiled=True)  12 us
    all_to_all x1, waiting for transfers between devices, exchange(): lax.all_to_all(operand, AXES, split_axis=0, concat_axis=0, tiled=True)  10 us
    pallas_call x1, Pallas kernels, convolve(): pl.pallas_call(lambda *refs: convolve_kernel(shape, plan, *refs), out_sha...  7.6 us
    pallas_call x1, Pallas kernels, unpack(): pl.pallas_call(lambda *refs: unpack_kernel(seq_len, *refs), grid=(channel...  2.5 us
    pallas_call x1, Pallas kernels, pack(): pl.pallas_call(lambda *refs: pack_kernel(share, parts, plan, *refs), grid...  2.48 us
  transfers between devices with their start and end apart: 1, of which 1 were waited for; matrix products, arithmetic and copies ran while one was open for 0% of the time, Pallas kernels for 0%

profile of v4, /device:TPU:1, one launch (start us, length us, event | category | flops | bytes accessed | tf_op | source)
XLA Modules:
  0.0 93.7 jit_solution(3688413456878943712)
XLA Ops:
  0.6 90.5 %conditional.1 = (f32[32,96,128]{2,1,0:T(8,128)S(1)}) conditional(s32[]{:T(128)} %convert_element_type.3, (bf16[128,1024]{1,0:T(8,128)(2,1)}, bf16[128,1024]{1,0:T(8,128)(2,1)}, bf16[128,1024]{1,0:T(8,128)(2,1)}, bf16[128,1024]{1,0:T(8,128)(2,1)}, bf16[128,1024]{1,0:T(8,128)(2,1)}, /*index=5*/bf16[17,256,256]{2,1,0:T(8,128)(2,1)}, ...), branch_computations={%region_0.1_spmd, %region_1.2_spmd} | conditional | bytes 23593024 | solution.py:329
  0.7 2.5 %pack.2 = (f32[32,16,128]{2,1,0:T(8,128)}, f32[32,64,128]{2,1,0:T(8,128)}) custom-call(bf16[128,1024]{1,0:T(8,128)(2,1)} %get-tuple-element.20.refs_0_, bf16[128,1024]{1,0:T(8,128)(2,1)} %get-tuple-element.32.refs_1_, bf16[128,1024]{1,0:T(8,128)(2,1)} %get-tuple-element.33.refs_2_, bf16[128,1024]{1,0:T(8,128)(2,1)} %get-tuple-element.34.refs_3_, ...), custom_call_target="tpu_custom_call" | custom-call | tf_op jit(solution)/shard_map/cond/branch_0_fun/pack/pallas_call | solution.py:258
  3.1 0.0 copy-start
  3.1 12.0 %all-to-all-start = ((f32[32,16,128]{2,1,0:T(8,128)}), f32[32,16,128]{2,1,0:T(8,128)S(1)}, u32[]{:S(2)}, u32[]{:S(2)}) async-start(f32[32,16,128]{2,1,0:T(8,128)} %get-tuple-element.36), calls=%async_computation | async-start | bytes 524288 | tf_op jit(solution)/shard_map/cond/branch_0_fun/all_to_all | solution.py:317
  15.1 10.0 %all-to-all-done.refs_0_ = f32[32,16,128]{2,1,0:T(8,128)S(1)} async-done(((f32[32,16,128]{2,1,0:T(8,128)}), f32[32,16,128]{2,1,0:T(8,128)S(1)}, u32[]{:S(2)}, u32[]{:S(2)}) %all-to-all-start) | async-done | bytes 262176 | tf_op jit(solution)/shard_map/cond/branch_0_fun/all_to_all | solution.py:317
  25.1 24.0 %all_to_all.20.refs_1_ = f32[32,64,128]{2,1,0:T(8,128)S(1)} all-to-all(f32[32,64,128]{2,1,0:T(8,128)} %get-tuple-element.37), channel_id=1, replica_groups=mesh['dp'=2,'tensor'=8,'line'=2,'column'=8] {'line','dp','column'}, dimensions={0} | all-to-all | bytes 2097152 | tf_op jit(solution)/shard_map/cond/branch_0_fun/all_to_all | solution.py:317
  49.2 0.0 copy-done
  49.2 7.6 %convolve.2 = f32[32,96,128]{2,1,0:T(8,128)S(1)} custom-call(f32[32,16,128]{2,1,0:T(8,128)S(1)} %all-to-all-done.refs_0_, f32[32,64,128]{2,1,0:T(8,128)S(1)} %all_to_all.20.refs_1_, bf16[17,256,256]{2,1,0:T(8,128)(2,1)} %get-tuple-element.38.refs_2_, bf16[17,256,256]{2,1,0:T(8,128)(2,1)S(1)} %copy-done), custom_call_target="tpu_custom_call" | custom-call | tf_op jit(solution)/shard_map/cond/branch_0_fun/convolve/pallas_call | solution.py:273
  56.8 34.4 %all_to_all.21 = f32[32,96,128]{2,1,0:T(8,128)S(1)} all-to-all(f32[32,96,128]{2,1,0:T(8,128)S(1)} %convolve.2), channel_id=1, replica_groups=mesh['dp'=2,'tensor'=8,'line'=2,'column'=8] {'line','dp','column'}, dimensions={0} | all-to-all | bytes 3145728 | tf_op jit(solution)/shard_map/cond/branch_0_fun/all_to_all | solution.py:317
  91.2 2.5 %unpack.1 = (bf16[128,1024]{1,0:T(8,128)(2,1)}, bf16[128,1024]{1,0:T(8,128)(2,1)}, bf16[128,1024]{1,0:T(8,128)(2,1)}, f32[128,1024]{1,0:T(8,128)}) custom-call(f32[32,96,128]{2,1,0:T(8,128)S(1)} %get-tuple-element.51.refs_0_, bf16[128,1024]{1,0:T(8,128)(2,1)} %refs_1_.1, bf16[128,1024]{1,0:T(8,128)(2,1)} %refs_2_.1, f32[1,1024]{1,0:T(1,128)} %bitcast.1, ...), custom_call_target="tpu_custom_call" | custom-call | tf_op jit(solution)/shard_map/unpack/pallas_call | solution.py:291
Async XLA Ops:
  3.1 46.0 %copy-start = (bf16[17,256,256]{2,1,0:T(8,128)(2,1)S(1)}, bf16[17,256,256]{2,1,0:T(8,128)(2,1)}, u32[]{:S(2)}) copy-start(bf16[17,256,256]{2,1,0:T(8,128)(2,1)} %get-tuple-element.39.refs_3_) | copy-start | bytes 6684676 | tf_op jit(solution)/shard_map/cond
  3.1 22.0 %all-to-all-start = ((f32[32,16,128]{2,1,0:T(8,128)}), f32[32,16,128]{2,1,0:T(8,128)S(1)}, u32[]{:S(2)}, u32[]{:S(2)}) async-start(f32[32,16,128]{2,1,0:T(8,128)} %get-tuple-element.36), calls=%async_computation | async-start | bytes 524288 | tf_op jit(solution)/shard_map/cond/branch_0_fun/all_to_all | solution.py:317

commit v5 on v4

--- a/solution.py
+++ b/solution.py
@@ -139,24 +139,26 @@
     return share // parts if signal == FILTER else share
 
 
-def pack_kernel(share, parts, plan, gate_in, values_in, long_filter, grad_out, gate_out, *packed):
-    mixed = gate_in[...].astype(jnp.float32) * values_in[...].astype(jnp.float32)
-    grad = grad_out[...].astype(jnp.float32) * gate_out[...].astype(jnp.float32)
-    signals = {MIXED: mixed, FILTER: long_filter[...].astype(jnp.float32), GRAD: grad}
+def pack_kernel(share, parts, members, *refs):
+    packed = refs[-1]
     part = lax.axis_index("dp")
-    for out, members in zip(packed, plan):
-        given = 0
-        for signal in members:
-            count = rows_of(signal, share, parts)
-            for lane in range(0, mixed.shape[1], LANES):
-                turned = signals[signal][:, lane:lane + LANES].T
-                for b in range(LANES // share):
-                    kept = turned[b * share:b * share + count]
-                    for other in range(1, share // count):
-                        start = b * share + other * count
-                        kept = jnp.where(part == other, turned[start:start + count], kept)
-                    out[lane // share + b, given:given + count, :] = kept
-            given += count
+    used = given = 0
+    for signal in members:
+        factors = refs[used:used + FACTORS[signal]]
+        used += FACTORS[signal]
+        count = rows_of(signal, share, parts)
+        for lane in range(0, packed.shape[0] * share, LANES):
+            value = factors[0][:, lane:lane + LANES].astype(jnp.float32)
+            for factor in factors[1:]:
+                value *= factor[:, lane:lane + LANES].astype(jnp.float32)
+            turned = value.T
+            for b in range(LANES // share):
+                kept = turned[b * share:b * share + count]
+                for other in range(1, share // count):
+                    start = b * share + other * count
+                    kept = jnp.where(part == other, turned[start:start + count], kept)
+                packed[lane // share + b, given:given + count, :] = kept
+        given += count
 
 
 def convolve_kernel(shape, plan, *refs):
@@ -250,19 +252,20 @@
         grad_filter[:, at] = turned(2) * (1.0 / math.sqrt(seq_len))
 
 
-def pack(width, devices, parts, plan, gate_in, values_in, long_filter, grad_out, gate_out):
-    tokens, channels = gate_in.shape
+def pack(width, devices, parts, members, signals):
+    operands = [factor for signal in members for factor in signals[signal]]
+    tokens, channels = operands[0].shape
     share = channels // devices
-    rows = [sum(rows_of(signal, share, parts) for signal in members) for members in plan]
-    plain = pl.BlockSpec((tokens, width), lambda i: (0, i))
+    rows = sum(rows_of(signal, share, parts) for signal in members)
     return pl.pallas_call(
-        lambda *refs: pack_kernel(share, parts, plan, *refs),
+        lambda *refs: pack_kernel(share, parts, members, *refs),
         grid=(channels // width,),
-        in_specs=[plain] * 5,
-        out_specs=[pl.BlockSpec((width // share, r, tokens), lambda i: (i, 0, 0)) for r in rows],
-        out_shape=[jax.ShapeDtypeStruct((devices, r, tokens), jnp.float32) for r in rows],
+        in_specs=[pl.BlockSpec((tokens, width), lambda i: (0, i))] * len(operands),
+        out_specs=pl.BlockSpec((width // share, rows, tokens), lambda i: (i, 0, 0)),
+        out_shape=jax.ShapeDtypeStruct((devices, rows, tokens), jnp.float32),
+        compiler_params=pltpu.CompilerParams(vmem_limit_bytes=16 * 1024 * 1024),
         name="pack",
-    )(gate_in, values_in, long_filter, grad_out, gate_out)
+    )(*operands)
 
 
 def convolve(shape, share, plan, received, high, low):
@@ -277,7 +280,7 @@
         out_specs=pl.BlockSpec(memory_space=pltpu.VMEM),
         scratch_shapes=[pltpu.VMEM((blocks + 1, forward_rows, 2 * LANES), jnp.float32),
                         pltpu.VMEM((blocks + 1, inverse_rows, 2 * LANES), jnp.float32)],
-        compiler_params=pltpu.CompilerParams(vmem_limit_bytes=40 * 1024 * 1024),
+        compiler_params=pltpu.CompilerParams(vmem_limit_bytes=24 * 1024 * 1024),
         name="convolve",
     )(*received, high, low)
 
@@ -295,6 +298,7 @@
                   pl.BlockSpec((1, width), lambda i: (0, i)), plain, plain],
         out_specs=[plain] * 4,
         out_shape=wide + [jax.ShapeDtypeStruct((tokens, channels), jnp.float32)],
+        compiler_params=pltpu.CompilerParams(vmem_limit_bytes=16 * 1024 * 1024),
         name="unpack",
     )(returned, gate_in, values_in, skip_gain[None, :], grad_out, gate_out))
 
@@ -302,6 +306,7 @@
 PACK_WIDTH = 512
 UNPACK_WIDTH = 512
 MIXED, FILTER, GRAD = 0, 1, 2
+FACTORS = (2, 1, 2)
 WHOLE = ((MIXED, FILTER, GRAD),)
 FILTER_FIRST = ((FILTER,), (MIXED, GRAD))
 
@@ -317,19 +322,21 @@
         return lax.all_to_all(operand, AXES, split_axis=0, concat_axis=0, tiled=True)
 
     def there_and_back(plan):
-        def run(*operands):
-            packed = pack(PACK_WIDTH, devices, shape[1], plan, *operands)
-            received = [exchange(packed[0])]
-            for part in packed[1:]:
-                part, _ = lax.optimization_barrier((part, received[-1][0, 0, 0]))
+        def run(gate_out, gate_in, values_in, long_filter, skip_gain, grad_out):
+            signals = {MIXED: (gate_in, values_in), FILTER: (long_filter,), GRAD: (grad_out, gate_out)}
+            received = []
+            for members in plan:
+                part = pack(PACK_WIDTH, devices, shape[1], members, signals)
+                if received:
+                    part, _ = lax.optimization_barrier((part, received[-1][0, 0, 0]))
                 received.append(exchange(part))
-            return exchange(convolve(shape, channels // devices, plan, received, high, low))
+            returned = exchange(convolve(shape, channels // devices, plan, received, high, low))
+            return unpack(UNPACK_WIDTH, tokens * blocks, returned, gate_in, values_in, skip_gain, grad_out, gate_out)
         return run
 
-    returned = lax.cond(
+    return lax.cond(
         lax.axis_index("tensor") % 2 == 0, there_and_back(WHOLE), there_and_back(FILTER_FIRST),
-        gate_in, values_in, long_filter, grad_out, gate_out)
-    return unpack(UNPACK_WIDTH, tokens * blocks, returned, gate_in, values_in, skip_gain, grad_out, gate_out)
+        gate_out, gate_in, values_in, long_filter, skip_gain, grad_out)
 
 
 def solution(mesh):

time: 94.1 us -> 92.5 us (0.983)
  waiting for transfers between devices: 10 us -> 8.34 us
    all_to_all x1, waiting for transfers between devices: 10 us -> 8.34 us  [exchange(): lax.all_to_all(operand, AXES, split_axis=0, concat_axis=0, tiled=True)]
    pallas_call x1 -> x2, Pallas kernels: 2.48 us -> 3.49 us  [pack(): pl.pallas_call(lambda *refs: pack_kernel(share, parts, members, *refs), g...]
    pallas_call x1, Pallas kernels: 2.5 us -> 1.52 us  [unpack(): pl.pallas_call(lambda *refs: unpack_kernel(seq_len, *refs), grid=(channel...]
  transfers between devices with their start and end apart: 1 -> 1, of which waited for: 1 -> 1; matrix products, arithmetic and copies ran while one was open for 0% -> 0% of each run, Pallas kernels for 0% -> 2%
where the time goes in v5:
time: 92.5 us; the launch traced here: 92.2 us
  blocking collectives  58.6 us (63%)
  Pallas kernels  12.6 us (14%)
  starting transfers between devices  11.9 us (13%)
  waiting for transfers between devices  8.34 us (9%)
    all_to_all x2, blocking collectives, exchange(): lax.all_to_all(operand, AXES, split_axis=0, concat_axis=0, tiled=True)  58.6 us
    all_to_all x1, starting transfers between devices, exchange(): lax.all_to_all(operand, AXES, split_axis=0, concat_axis=0, tiled=True)  11.9 us
    all_to_all x1, waiting for transfers between devices, exchange(): lax.all_to_all(operand, AXES, split_axis=0, concat_axis=0, tiled=True)  8.34 us
    pallas_call x1, Pallas kernels, convolve(): pl.pallas_call(lambda *refs: convolve_kernel(shape, plan, *refs), out_sha...  7.59 us
    pallas_call x2, Pallas kernels, pack(): pl.pallas_call(lambda *refs: pack_kernel(share, parts, members, *refs), g...  3.49 us
  transfers between devices with their start and end apart: 1, of which 1 were waited for; matrix products, arithmetic and copies ran while one was open for 0% of the time, Pallas kernels for 2%

profile of v5, /device:TPU:1, one launch (start us, length us, event | category | flops | bytes accessed | tf_op | source)
XLA Modules:
  0.0 92.2 jit_solution(13725894600116028437)
XLA Ops:
  0.6 91.5 %conditional.1 = ((bf16[128,1024]{1,0:T(8,128)(2,1)}, bf16[128,1024]{1,0:T(8,128)(2,1)}, bf16[128,1024]{1,0:T(8,128)(2,1)}, f32[128,1024]{1,0:T(8,128)})) conditional(s32[]{:T(128)} %convert_element_type.3, (bf16[128,1024]{1,0:T(8,128)(2,1)}, bf16[128,1024]{1,0:T(8,128)(2,1)}, bf16[128,1024]{1,0:T(8,128)(2,1)}, bf16[128,1024]{1,0:T(8,128)(2,1)}, ...), branch_computations={%region_0.1_spmd, %region_1.2_spmd} | conditional | bytes 27803852 | solution.py:337
  0.7 1.8 %pack.3 = f32[32,16,128]{2,1,0:T(8,128)} custom-call(bf16[128,1024]{1,0:T(8,128)(2,1)} %get-tuple-element.32.refs_0_), custom_call_target="tpu_custom_call" | custom-call | tf_op jit(solution)/shard_map/cond/branch_0_fun/pack/pallas_call | solution.py:260
  2.4 11.9 %all-to-all-start = ((f32[32,16,128]{2,1,0:T(8,128)}), f32[32,16,128]{2,1,0:T(8,128)S(1)}, u32[]{:S(2)}, u32[]{:S(2)}) async-start(f32[32,16,128]{2,1,0:T(8,128)} %pack.3), calls=%async_computation | async-start | bytes 524288 | tf_op jit(solution)/shard_map/cond/branch_0_fun/all_to_all | solution.py:322
  14.3 0.0 copy-start
  14.3 1.7 %pack.4 = f32[32,64,128]{2,1,0:T(8,128)S(1)} custom-call(bf16[128,1024]{1,0:T(8,128)(2,1)} %get-tuple-element.33.refs_0_.refs_1_, bf16[128,1024]{1,0:T(8,128)(2,1)} %get-tuple-element.34.refs_1_.refs_2_, bf16[128,1024]{1,0:T(8,128)(2,1)} %get-tuple-element.35.refs_2_.refs_4_, bf16[128,1024]{1,0:T(8,128)(2,1)} %get-tuple-element.36.refs_3_.refs_5_), custom_call_target="tpu_custom_call" | custom-call | tf_op jit(solution)/shard_map/cond/branch_0_fun/pack/pallas_call | solution.py:260
  16.0 8.3 %all-to-all-done.refs_0_ = f32[32,16,128]{2,1,0:T(8,128)S(1)} async-done(((f32[32,16,128]{2,1,0:T(8,128)}), f32[32,16,128]{2,1,0:T(8,128)S(1)}, u32[]{:S(2)}, u32[]{:S(2)}) %all-to-all-start) | async-done | bytes 262176 | tf_op jit(solution)/shard_map/cond/branch_0_fun/all_to_all | solution.py:322
  24.4 23.7 %all_to_all.20.refs_1_ = f32[32,64,128]{2,1,0:T(8,128)S(1)} all-to-all(f32[32,64,128]{2,1,0:T(8,128)S(1)} %pack.4), channel_id=1, replica_groups=mesh['dp'=2,'tensor'=8,'line'=2,'column'=8] {'line','dp','column'}, dimensions={0} | all-to-all | bytes 2097152 | tf_op jit(solution)/shard_map/cond/branch_0_fun/all_to_all | solution.py:322
  48.1 0.0 copy-done
  48.1 7.6 %convolve.2 = f32[32,96,128]{2,1,0:T(8,128)S(1)} custom-call(f32[32,16,128]{2,1,0:T(8,128)S(1)} %all-to-all-done.refs_0_, f32[32,64,128]{2,1,0:T(8,128)S(1)} %all_to_all.20.refs_1_, bf16[17,256,256]{2,1,0:T(8,128)(2,1)} %get-tuple-element.37.refs_2_, bf16[17,256,256]{2,1,0:T(8,128)(2,1)S(1)} %copy-done), custom_call_target="tpu_custom_call" | custom-call | tf_op jit(solution)/shard_map/cond/branch_0_fun/convolve/pallas_call | solution.py:276
  55.7 0.0 copy-start.3
  55.7 0.0 copy-start.5
  55.7 0.0 copy-start.7
  55.7 0.0 copy-start.9
  55.8 0.0 copy-start.11
  55.8 34.9 %all_to_all.21.refs_0_ = f32[32,96,128]{2,1,0:T(8,128)S(1)} all-to-all(f32[32,96,128]{2,1,0:T(8,128)S(1)} %convolve.2), channel_id=1, replica_groups=mesh['dp'=2,'tensor'=8,'line'=2,'column'=8] {'line','dp','column'}, dimensions={0} | all-to-all | bytes 3145728 | tf_op jit(solution)/shard_map/cond/branch_0_fun/all_to_all | solution.py:322
  90.6 0.0 copy-done.3
  90.6 0.0 copy-done.5
  90.6 0.0 copy-done.7
  90.6 0.0 copy-done.9
  90.7 0.0 copy-done.11
  90.7 1.5 %unpack.2 = (bf16[128,1024]{1,0:T(8,128)(2,1)}, bf16[128,1024]{1,0:T(8,128)(2,1)}, bf16[128,1024]{1,0:T(8,128)(2,1)}, f32[128,1024]{1,0:T(8,128)}) custom-call(f32[32,96,128]{2,1,0:T(8,128)S(1)} %all_to_all.21.refs_0_, bf16[128,1024]{1,0:T(8,128)(2,1)S(1)} %copy-done.3, bf16[128,1024]{1,0:T(8,128)(2,1)S(1)} %copy-done.5, f32[1,1024]{1,0:T(1,128)S(1)} %bitcast.2, ...), custom_call_target="tpu_custom_call" | custom-call | tf_op jit(solution)/shard_map/cond/branch_0_fun/unpack/pallas_call | solution.py:294
Async XLA Ops:
  2.4 21.9 %all-to-all-start = ((f32[32,16,128]{2,1,0:T(8,128)}), f32[32,16,128]{2,1,0:T(8,128)S(1)}, u32[]{:S(2)}, u32[]{:S(2)}) async-start(f32[32,16,128]{2,1,0:T(8,128)} %pack.3), calls=%async_computation | async-start | bytes 524288 | tf_op jit(solution)/shard_map/cond/branch_0_fun/all_to_all | solution.py:322
  14.3 33.8 %copy-start = (bf16[17,256,256]{2,1,0:T(8,128)(2,1)S(1)}, bf16[17,256,256]{2,1,0:T(8,128)(2,1)}, u32[]{:S(2)}) copy-start(bf16[17,256,256]{2,1,0:T(8,128)(2,1)} %get-tuple-element.38.refs_3_) | copy-start | bytes 6684676 | tf_op jit(solution)/shard_map/cond
  55.7 34.9 %copy-start.3 = (bf16[128,1024]{1,0:T(8,128)(2,1)S(1)}, bf16[128,1024]{1,0:T(8,128)(2,1)}, u32[]{:S(2)}) copy-start(bf16[128,1024]{1,0:T(8,128)(2,1)} %get-tuple-element.33.refs_0_.refs_1_) | copy-start | bytes 786436 | tf_op jit(solution)/shard_map/cond
  55.7 34.9 %copy-start.5 = (bf16[128,1024]{1,0:T(8,128)(2,1)S(1)}, bf16[128,1024]{1,0:T(8,128)(2,1)}, u32[]{:S(2)}) copy-start(bf16[128,1024]{1,0:T(8,128)(2,1)} %get-tuple-element.34.refs_1_.refs_2_) | copy-start | bytes 786436 | tf_op jit(solution)/shard_map/cond
  55.7 34.9 %copy-start.7 = (bf16[128,1024]{1,0:T(8,128)(2,1)S(1)}, bf16[128,1024]{1,0:T(8,128)(2,1)}, u32[]{:S(2)}) copy-start(bf16[128,1024]{1,0:T(8,128)(2,1)} %get-tuple-element.35.refs_2_.refs_4_) | copy-start | bytes 786436 | tf_op jit(solution)/shard_map/cond
  55.7 34.9 %copy-start.9 = (bf16[128,1024]{1,0:T(8,128)(2,1)S(1)}, bf16[128,1024]{1,0:T(8,128)(2,1)}, u32[]{:S(2)}) copy-start(bf16[128,1024]{1,0:T(8,128)(2,1)} %get-tuple-element.36.refs_3_.refs_5_) | copy-start | bytes 786436 | tf_op jit(solution)/shard_map/cond
  55.8 34.9 %copy-start.11 = (f32[1024]{0:T(1024)S(1)}, f32[1024]{0:T(1024)}, u32[]{:S(2)}) copy-start(f32[1024]{0:T(1024)} %get-tuple-element.39) | copy-start | bytes 12292 | tf_op jit(solution)/shard_map/cond

commit v6 on v5

--- a/solution.py
+++ b/solution.py
@@ -107,19 +107,17 @@
     return front + [evens[p] - odd_part[p] for p in range(half)]
 
 
-def table(blocks):
+def tables(blocks):
     rows_all = 2 * blocks
-    length = rows_all * LANES
     lane = np.arange(LANES)
-    out = []
-    for k1 in range(blocks + 1):
-        angles = 2.0 * np.pi * (lane[:, None] * (k1 + rows_all * lane[None, :]) % length) / length
-        cosine, sine = np.cos(angles), np.sin(angles)
-        out.append(np.block([[cosine, -sine], [sine, cosine]]))
-    whole = np.stack(out).astype(np.float32)
+    angles = 2.0 * np.pi * (lane[:, None] * lane[None, :] % LANES) / LANES
+    cosine, sine = np.cos(angles), np.sin(angles)
+    whole = np.block([[cosine, -sine], [sine, cosine]]).astype(np.float32)
     high = whole.astype(jnp.bfloat16)
     low = (whole - high.astype(np.float32)).astype(jnp.bfloat16)
-    return high, low
+    turn = 2.0 * np.pi * np.arange(blocks + 1)[:, None] * lane[None, :] / (rows_all * LANES)
+    twiddles = np.stack([np.cos(turn), np.sin(turn)], axis=1).astype(np.float32)
+    return high, low, np.repeat(twiddles[:, :, None, :], 8, axis=2)
 
 
 def split(value):
@@ -162,7 +160,7 @@
 
 
 def convolve_kernel(shape, plan, *refs):
-    received, (high, low, result, spectrum, inverted) = refs[:len(plan)], refs[len(plan):]
+    received, (high, low, twiddles, result, spectrum, inverted) = refs[:len(plan)], refs[len(plan):]
     lines, parts, columns = shape
     blocks = lines * columns
     share = result.shape[1] // 3
@@ -189,38 +187,52 @@
                         rows_all)
                     for k1 in range(blocks + 1):
                         re, im = out[k1]
-                        spectrum[k1, given, :LANES] = re
-                        spectrum[k1, given, LANES:] = jnp.zeros_like(re) if im is None else im
+                        cosine, sine = twiddles[k1, 0], twiddles[k1, 1]
+                        if im is None:
+                            spectrum[k1, given, :LANES] = re * cosine
+                            spectrum[k1, given, LANES:] = re * -sine
+                        else:
+                            spectrum[k1, given, :LANES] = re * cosine + im * sine
+                            spectrum[k1, given, LANES:] = im * cosine - re * sine
                     return carry
 
                 lax.fori_loop(0, count // 8, forward, 0)
             taken_row += count
 
-    for k1 in range(blocks + 1):
-        freq = dot_parts(spectrum[k1], high[k1], low[k1], 0)
-        factor = scale * 0.5 if k1 in (0, blocks) else scale
-        filt_re, filt_im = freq[filt_row:, :LANES], freq[filt_row:, LANES:]
-        filt_re, filt_im = filt_re * factor, filt_im * factor
+    rows, products_rows = spectrum.shape[1], inverted.shape[1]
+    for begin in range(0, blocks + 1, GROUP):
+        end = min(begin + GROUP, blocks + 1)
+        freqs = dot_parts(spectrum[begin:end].reshape((end - begin) * rows, 2 * LANES), high[...], low[...], 0)
         products = []
-        for part in range(parts):
-            mixed = slice(part * share, (part + 1) * share)
-            grad = slice(grad_row + part * share, grad_row + (part + 1) * share)
-            mixed_re, mixed_im = freq[mixed, :LANES], freq[mixed, LANES:]
-            grad_re, grad_im = freq[grad, :LANES], freq[grad, LANES:]
-            products.append(jnp.concatenate([
-                filt_re * mixed_re - filt_im * mixed_im, filt_re * mixed_im + filt_im * mixed_re], axis=1))
-            products.append(jnp.concatenate([
-                filt_re * grad_re + filt_im * grad_im, filt_re * grad_im - filt_im * grad_re], axis=1))
-            mixed_re, mixed_im = mixed_re * factor, mixed_im * factor
-            products.append(jnp.concatenate([
-                mixed_re * grad_re + mixed_im * grad_im, mixed_re * grad_im - mixed_im * grad_re], axis=1))
-        inverted[k1] = dot_parts(jnp.concatenate(products, axis=0), high[k1], low[k1], 1)
+        for k1 in range(begin, end):
+            freq = freqs[(k1 - begin) * rows:(k1 - begin + 1) * rows]
+            factor = scale * 0.5 if k1 in (0, blocks) else scale
+            filt_re, filt_im = freq[filt_row:, :LANES], freq[filt_row:, LANES:]
+            filt_re, filt_im = filt_re * factor, filt_im * factor
+            for part in range(parts):
+                mixed = slice(part * share, (part + 1) * share)
+                grad = slice(grad_row + part * share, grad_row + (part + 1) * share)
+                mixed_re, mixed_im = freq[mixed, :LANES], freq[mixed, LANES:]
+                grad_re, grad_im = freq[grad, :LANES], freq[grad, LANES:]
+                products.append(jnp.concatenate([
+                    filt_re * mixed_re - filt_im * mixed_im, filt_re * mixed_im + filt_im * mixed_re], axis=1))
+                products.append(jnp.concatenate([
+                    filt_re * grad_re + filt_im * grad_im, filt_re * grad_im - filt_im * grad_re], axis=1))
+                mixed_re, mixed_im = mixed_re * factor, mixed_im * factor
+                products.append(jnp.concatenate([
+                    mixed_re * grad_re + mixed_im * grad_im, mixed_re * grad_im - mixed_im * grad_re], axis=1))
+        back = dot_parts(jnp.concatenate(products, axis=0), high[...], low[...], 1)
+        inverted[begin:end] = back.reshape(end - begin, products_rows, 2 * LANES)
 
     for part in range(parts):
         def backward(tile, carry):
             start = pl.multiple_of(tile * 8, 8)
             at = pl.ds(pl.multiple_of(part * 3 * share + start, 8), 8)
-            spec = {k1: (inverted[k1, at, :LANES], inverted[k1, at, LANES:]) for k1 in range(blocks + 1)}
+            spec = {}
+            for k1 in range(blocks + 1):
+                re, im = inverted[k1, at, :LANES], inverted[k1, at, LANES:]
+                cosine, sine = twiddles[k1, 0], twiddles[k1, 1]
+                spec[k1] = (re * cosine - im * sine, re * sine + im * cosine)
             values = real_inverse(spec, rows_all, True)
             for x in range(lines):
                 for z in range(columns):
@@ -268,7 +280,7 @@
     )(*operands)
 
 
-def convolve(shape, share, plan, received, high, low):
+def convolve(shape, share, plan, received, constants):
     devices, _, tokens = received[0].shape
     blocks = shape[0] * shape[2]
     forward_rows = (2 * shape[1] + 1) * share
@@ -276,13 +288,13 @@
     return pl.pallas_call(
         lambda *refs: convolve_kernel(shape, plan, *refs),
         out_shape=jax.ShapeDtypeStruct((devices, 3 * share, tokens), jnp.float32),
-        in_specs=[pl.BlockSpec(memory_space=pltpu.VMEM)] * (len(plan) + 2),
+        in_specs=[pl.BlockSpec(memory_space=pltpu.VMEM)] * (len(plan) + len(constants)),
         out_specs=pl.BlockSpec(memory_space=pltpu.VMEM),
         scratch_shapes=[pltpu.VMEM((blocks + 1, forward_rows, 2 * LANES), jnp.float32),
                         pltpu.VMEM((blocks + 1, inverse_rows, 2 * LANES), jnp.float32)],
         compiler_params=pltpu.CompilerParams(vmem_limit_bytes=24 * 1024 * 1024),
         name="convolve",
-    )(*received, high, low)
+    )(*received, *constants)
 
 
 def unpack(width, seq_len, returned, gate_in, values_in, skip_gain, grad_out, gate_out):
@@ -303,6 +315,7 @@
     )(returned, gate_in, values_in, skip_gain[None, :], grad_out, gate_out))
 
 
+GROUP = 3
 PACK_WIDTH = 512
 UNPACK_WIDTH = 512
 MIXED, FILTER, GRAD = 0, 1, 2
@@ -316,7 +329,7 @@
     shape = tuple(lax.axis_size(axis) for axis in AXES)
     devices = math.prod(shape)
     blocks = shape[0] * shape[2]
-    high, low = (jnp.asarray(t) for t in table(blocks))
+    constants = [jnp.asarray(t) for t in tables(blocks)]
 
     def exchange(operand):
         return lax.all_to_all(operand, AXES, split_axis=0, concat_axis=0, tiled=True)
@@ -330,7 +343,7 @@
                 if received:
                     part, _ = lax.optimization_barrier((part, received[-1][0, 0, 0]))
                 received.append(exchange(part))
-            returned = exchange(convolve(shape, channels // devices, plan, received, high, low))
+            returned = exchange(convolve(shape, channels // devices, plan, received, constants))
             return unpack(UNPACK_WIDTH, tokens * blocks, returned, gate_in, values_in, skip_gain, grad_out, gate_out)
         return run
 

time: 92.5 us -> 91.5 us (0.989)
  Pallas kernels: 12.6 us -> 10 us
  blocking collectives: 58.6 us -> 59.9 us
    pallas_call x1, Pallas kernels: 7.59 us -> 5.18 us  [convolve(): pl.pallas_call(lambda *refs: convolve_kernel(shape, plan, *refs), out_sha...]
    all_to_all x2, blocking collectives: 58.6 us -> 59.9 us  [exchange(): lax.all_to_all(operand, AXES, split_axis=0, concat_axis=0, tiled=True)]
where the time goes in v6:
time: 91.5 us; the launch traced here: 91.2 us
  blocking collectives  59.9 us (65%)
  starting transfers between devices  11.9 us (13%)
  Pallas kernels  10 us (11%)
  waiting for transfers between devices  8.64 us (9%)
    all_to_all x2, blocking collectives, exchange(): lax.all_to_all(operand, AXES, split_axis=0, concat_axis=0, tiled=True)  59.9 us
    all_to_all x1, starting transfers between devices, exchange(): lax.all_to_all(operand, AXES, split_axis=0, concat_axis=0, tiled=True)  11.9 us
    all_to_all x1, waiting for transfers between devices, exchange(): lax.all_to_all(operand, AXES, split_axis=0, concat_axis=0, tiled=True)  8.64 us
    pallas_call x1, Pallas kernels, convolve(): pl.pallas_call(lambda *refs: convolve_kernel(shape, plan, *refs), out_sha...  5.18 us
    pallas_call x2, Pallas kernels, pack(): pl.pallas_call(lambda *refs: pack_kernel(share, parts, members, *refs), g...  3.34 us
  transfers between devices with their start and end apart: 1, of which 1 were waited for; matrix products, arithmetic and copies ran while one was open for 0% of the time, Pallas kernels for 2%

profile of v6, /device:TPU:1, one launch (start us, length us, event | category | flops | bytes accessed | tf_op | source)
XLA Modules:
  0.0 91.2 jit_solution(7445299501252237157)
XLA Ops:
  0.6 90.6 %conditional.1 = ((bf16[128,1024]{1,0:T(8,128)(2,1)}, bf16[128,1024]{1,0:T(8,128)(2,1)}, bf16[128,1024]{1,0:T(8,128)(2,1)}, f32[128,1024]{1,0:T(8,128)})) conditional(s32[]{:T(128)} %convert_element_type.3, (bf16[128,1024]{1,0:T(8,128)(2,1)}, bf16[128,1024]{1,0:T(8,128)(2,1)}, bf16[128,1024]{1,0:T(8,128)(2,1)}, bf16[128,1024]{1,0:T(8,128)(2,1)}, ...), branch_computations={%region_0.1_spmd, %region_1.2_spmd} | conditional | bytes 11845896 | solution.py:350
  0.7 1.8 %pack.3 = f32[32,16,128]{2,1,0:T(8,128)} custom-call(bf16[128,1024]{1,0:T(8,128)(2,1)} %get-tuple-element.36.refs_0_), custom_call_target="tpu_custom_call" | custom-call | tf_op jit(solution)/shard_map/cond/branch_0_fun/pack/pallas_call | solution.py:272
  2.4 11.9 %all-to-all-start = ((f32[32,16,128]{2,1,0:T(8,128)}), f32[32,16,128]{2,1,0:T(8,128)S(1)}, u32[]{:S(2)}, u32[]{:S(2)}) async-start(f32[32,16,128]{2,1,0:T(8,128)} %pack.3), calls=%async_computation | async-start | bytes 524288 | tf_op jit(solution)/shard_map/cond/branch_0_fun/all_to_all | solution.py:335
  14.3 1.5 %pack.4 = f32[32,64,128]{2,1,0:T(8,128)S(1)} custom-call(bf16[128,1024]{1,0:T(8,128)(2,1)} %get-tuple-element.37.refs_0_.refs_1_, bf16[128,1024]{1,0:T(8,128)(2,1)} %get-tuple-element.38.refs_1_.refs_2_, bf16[128,1024]{1,0:T(8,128)(2,1)} %get-tuple-element.39.refs_2_.refs_4_, bf16[128,1024]{1,0:T(8,128)(2,1)} %get-tuple-element.40.refs_3_.refs_5_), custom_call_target="tpu_custom_call" | custom-call | tf_op jit(solution)/shard_map/cond/branch_0_fun/pack/pallas_call | solution.py:272
  15.9 0.0 copy-start.8
  15.9 0.0 copy-start.10
  15.9 0.0 copy-start.12
  15.9 8.6 %all-to-all-done.refs_0_ = f32[32,16,128]{2,1,0:T(8,128)S(1)} async-done(((f32[32,16,128]{2,1,0:T(8,128)}), f32[32,16,128]{2,1,0:T(8,128)S(1)}, u32[]{:S(2)}, u32[]{:S(2)}) %all-to-all-start) | async-done | bytes 262176 | tf_op jit(solution)/shard_map/cond/branch_0_fun/all_to_all | solution.py:335
  24.5 23.6 %all_to_all.20.refs_1_ = f32[32,64,128]{2,1,0:T(8,128)S(1)} all-to-all(f32[32,64,128]{2,1,0:T(8,128)S(1)} %pack.4), channel_id=1, replica_groups=mesh['dp'=2,'tensor'=8,'line'=2,'column'=8] {'line','dp','column'}, dimensions={0} | all-to-all | bytes 2097152 | tf_op jit(solution)/shard_map/cond/branch_0_fun/all_to_all | solution.py:335
  48.1 0.0 copy-done.8
  48.1 0.0 copy-done.10
  48.1 0.0 copy-done.12
  48.1 5.2 %convolve.2 = f32[32,96,128]{2,1,0:T(8,128)S(1)} custom-call(f32[32,16,128]{2,1,0:T(8,128)S(1)} %all-to-all-done.refs_0_, f32[32,64,128]{2,1,0:T(8,128)S(1)} %all_to_all.20.refs_1_, bf16[256,256]{1,0:T(8,128)(2,1)S(1)} %copy-done.12, bf16[256,256]{1,0:T(8,128)(2,1)S(1)} %copy-done.10, f32[17,2,8,128]{3,2,1,0:T(8,128)S(1)} %copy-done.8), custom_call_target="tpu_custom_call" | custom-call | tf_op jit(solution)/shard_map/cond/branch_0_fun/convolve/pallas_call | solution.py:288
  53.3 0.0 copy-start
  53.3 0.0 copy-start.2
  53.3 0.0 copy-start.4
  53.4 0.0 copy-start.6
  53.4 0.0 copy-start.14
  53.4 36.3 %all_to_all.21.refs_0_ = f32[32,96,128]{2,1,0:T(8,128)S(1)} all-to-all(f32[32,96,128]{2,1,0:T(8,128)S(1)} %convolve.2), channel_id=1, replica_groups=mesh['dp'=2,'tensor'=8,'line'=2,'column'=8] {'line','dp','column'}, dimensions={0} | all-to-all | bytes 3145728 | tf_op jit(solution)/shard_map/cond/branch_0_fun/all_to_all | solution.py:335
  89.7 0.0 copy-done
  89.7 0.0 copy-done.2
  89.7 0.0 copy-done.4
  89.7 0.0 copy-done.6
  89.7 0.0 copy-done.14
  89.7 1.5 %unpack.2 = (bf16[128,1024]{1,0:T(8,128)(2,1)}, bf16[128,1024]{1,0:T(8,128)(2,1)}, bf16[128,1024]{1,0:T(8,128)(2,1)}, f32[128,1024]{1,0:T(8,128)}) custom-call(f32[32,96,128]{2,1,0:T(8,128)S(1)} %all_to_all.21.refs_0_, bf16[128,1024]{1,0:T(8,128)(2,1)S(1)} %copy-done, bf16[128,1024]{1,0:T(8,128)(2,1)S(1)} %copy-done.2, f32[1,1024]{1,0:T(1,128)S(1)} %bitcast.2, ...), custom_call_target="tpu_custom_call" | custom-call | tf_op jit(solution)/shard_map/cond/branch_0_fun/unpack/pallas_call | solution.py:306
Async XLA Ops:
  2.4 22.1 %all-to-all-start = ((f32[32,16,128]{2,1,0:T(8,128)}), f32[32,16,128]{2,1,0:T(8,128)S(1)}, u32[]{:S(2)}, u32[]{:S(2)}) async-start(f32[32,16,128]{2,1,0:T(8,128)} %pack.3), calls=%async_computation | async-start | bytes 524288 | tf_op jit(solution)/shard_map/cond/branch_0_fun/all_to_all | solution.py:335
  15.9 32.3 %copy-start.8 = (f32[17,2,8,128]{3,2,1,0:T(8,128)S(1)}, f32[17,2,8,128]{3,2,1,0:T(8,128)}, u32[]{:S(2)}) copy-start(f32[17,2,8,128]{3,2,1,0:T(8,128)} %get-tuple-element.43.refs_4_) | copy-start | bytes 417796 | tf_op jit(solution)/shard_map/cond
  15.9 32.3 %copy-start.10 = (bf16[256,256]{1,0:T(8,128)(2,1)S(1)}, bf16[256,256]{1,0:T(8,128)(2,1)}, u32[]{:S(2)}) copy-start(bf16[256,256]{1,0:T(8,128)(2,1)} %get-tuple-element.42.refs_3_) | copy-start | bytes 393220 | tf_op jit(solution)/shard_map/cond
  15.9 32.2 %copy-start.12 = (bf16[256,256]{1,0:T(8,128)(2,1)S(1)}, bf16[256,256]{1,0:T(8,128)(2,1)}, u32[]{:S(2)}) copy-start(bf16[256,256]{1,0:T(8,128)(2,1)} %get-tuple-element.41.refs_2_) | copy-start | bytes 393220 | tf_op jit(solution)/shard_map/cond
  53.3 36.4 %copy-start = (bf16[128,1024]{1,0:T(8,128)(2,1)S(1)}, bf16[128,1024]{1,0:T(8,128)(2,1)}, u32[]{:S(2)}) copy-start(bf16[128,1024]{1,0:T(8,128)(2,1)} %get-tuple-element.37.refs_0_.refs_1_) | copy-start | bytes 786436 | tf_op jit(solution)/shard_map/cond
  53.3 36.4 %copy-start.2 = (bf16[128,1024]{1,0:T(8,128)(2,1)S(1)}, bf16[128,1024]{1,0:T(8,128)(2,1)}, u32[]{:S(2)}) copy-start(bf16[128,1024]{1,0:T(8,128)(2,1)} %get-tuple-element.38.refs_1_.refs_2_) | copy-start | bytes 786436 | tf_op jit(solution)/shard_map/cond
  53.3 36.4 %copy-start.4 = (bf16[128,1024]{1,0:T(8,128)(2,1)S(1)}, bf16[128,1024]{1,0:T(8,128)(2,1)}, u32[]{:S(2)}) copy-start(bf16[128,1024]{1,0:T(8,128)(2,1)} %get-tuple-element.39.refs_2_.refs_4_) | copy-start | bytes 786436 | tf_op jit(solution)/shard_map/cond
  53.4 36.3 %copy-start.6 = (bf16[128,1024]{1,0:T(8,128)(2,1)S(1)}, bf16[128,1024]{1,0:T(8,128)(2,1)}, u32[]{:S(2)}) copy-start(bf16[128,1024]{1,0:T(8,128)(2,1)} %get-tuple-element.40.refs_3_.refs_5_) | copy-start | bytes 786436 | tf_op jit(solution)/shard_map/cond
  53.4 36.3 %copy-start.14 = (f32[1024]{0:T(1024)S(1)}, f32[1024]{0:T(1024)}, u32[]{:S(2)}) copy-start(f32[1024]{0:T(1024)} %get-tuple-element.44) | copy-start | bytes 12292 | tf_op jit(solution)/shard_map/cond

commit v7 on v6

--- a/solution.py
+++ b/solution.py
@@ -196,7 +196,7 @@
                             spectrum[k1, given, LANES:] = im * cosine - re * sine
                     return carry
 
-                lax.fori_loop(0, count // 8, forward, 0)
+                lax.fori_loop(0, count // 8, forward, 0, unroll=True)
             taken_row += count
 
     rows, products_rows = spectrum.shape[1], inverted.shape[1]
@@ -239,7 +239,7 @@
                     result[source(x, part, z), pl.ds(start, 8), :] = values[x * columns + z]
             return carry
 
-        lax.fori_loop(0, 3 * share // 8, backward, 0)
+        lax.fori_loop(0, 3 * share // 8, backward, 0, unroll=True)
 
 
 def unpack_kernel(seq_len, returned, gate_in, values_in, skip_gain, grad_out, gate_out,

time: 91.5 us -> 90.6 us (level)
  no operation moved by 1% of the time
where the time goes in v7:
time: 90.6 us; the launch traced here: 90.4 us
  blocking collectives  59.9 us (66%)
  starting transfers between devices  11.9 us (13%)
  Pallas kernels  9.18 us (10%)
  waiting for transfers between devices  8.64 us (10%)
    all_to_all x2, blocking collectives, exchange(): lax.all_to_all(operand, AXES, split_axis=0, concat_axis=0, tiled=True)  59.9 us
    all_to_all x1, starting transfers between devices, exchange(): lax.all_to_all(operand, AXES, split_axis=0, concat_axis=0, tiled=True)  11.9 us
    all_to_all x1, waiting for transfers between devices, exchange(): lax.all_to_all(operand, AXES, split_axis=0, concat_axis=0, tiled=True)  8.64 us
    pallas_call x1, Pallas kernels, convolve(): pl.pallas_call(lambda *refs: convolve_kernel(shape, plan, *refs), out_sha...  4.32 us
    pallas_call x2, Pallas kernels, pack(): pl.pallas_call(lambda *refs: pack_kernel(share, parts, members, *refs), g...  3.34 us
  transfers between devices with their start and end apart: 1, of which 1 were waited for; matrix products, arithmetic and copies ran while one was open for 0% of the time, Pallas kernels for 2%

profile of v7, /device:TPU:1, one launch (start us, length us, event | category | flops | bytes accessed | tf_op | source)
XLA Modules:
  0.0 90.4 jit_solution(17372209743703455847)
XLA Ops:
  0.6 89.7 %conditional.1 = ((bf16[128,1024]{1,0:T(8,128)(2,1)}, bf16[128,1024]{1,0:T(8,128)(2,1)}, bf16[128,1024]{1,0:T(8,128)(2,1)}, f32[128,1024]{1,0:T(8,128)})) conditional(s32[]{:T(128)} %convert_element_type.3, (bf16[128,1024]{1,0:T(8,128)(2,1)}, bf16[128,1024]{1,0:T(8,128)(2,1)}, bf16[128,1024]{1,0:T(8,128)(2,1)}, bf16[128,1024]{1,0:T(8,128)(2,1)}, ...), branch_computations={%region_0.1_spmd, %region_1.2_spmd} | conditional | bytes 11845896 | solution.py:350
  0.7 1.8 %pack.3 = f32[32,16,128]{2,1,0:T(8,128)} custom-call(bf16[128,1024]{1,0:T(8,128)(2,1)} %get-tuple-element.36.refs_0_), custom_call_target="tpu_custom_call" | custom-call | tf_op jit(solution)/shard_map/cond/branch_0_fun/pack/pallas_call | solution.py:272
  2.4 11.9 %all-to-all-start = ((f32[32,16,128]{2,1,0:T(8,128)}), f32[32,16,128]{2,1,0:T(8,128)S(1)}, u32[]{:S(2)}, u32[]{:S(2)}) async-start(f32[32,16,128]{2,1,0:T(8,128)} %pack.3), calls=%async_computation | async-start | bytes 524288 | tf_op jit(solution)/shard_map/cond/branch_0_fun/all_to_all | solution.py:335
  14.3 1.5 %pack.4 = f32[32,64,128]{2,1,0:T(8,128)S(1)} custom-call(bf16[128,1024]{1,0:T(8,128)(2,1)} %get-tuple-element.37.refs_0_.refs_1_, bf16[128,1024]{1,0:T(8,128)(2,1)} %get-tuple-element.38.refs_1_.refs_2_, bf16[128,1024]{1,0:T(8,128)(2,1)} %get-tuple-element.39.refs_2_.refs_4_, bf16[128,1024]{1,0:T(8,128)(2,1)} %get-tuple-element.40.refs_3_.refs_5_), custom_call_target="tpu_custom_call" | custom-call | tf_op jit(solution)/shard_map/cond/branch_0_fun/pack/pallas_call | solution.py:272
  15.9 0.0 copy-start.8
  15.9 0.0 copy-start.10
  15.9 0.0 copy-start.12
  15.9 8.6 %all-to-all-done.refs_0_ = f32[32,16,128]{2,1,0:T(8,128)S(1)} async-done(((f32[32,16,128]{2,1,0:T(8,128)}), f32[32,16,128]{2,1,0:T(8,128)S(1)}, u32[]{:S(2)}, u32[]{:S(2)}) %all-to-all-start) | async-done | bytes 262176 | tf_op jit(solution)/shard_map/cond/branch_0_fun/all_to_all | solution.py:335
  24.5 23.6 %all_to_all.20.refs_1_ = f32[32,64,128]{2,1,0:T(8,128)S(1)} all-to-all(f32[32,64,128]{2,1,0:T(8,128)S(1)} %pack.4), channel_id=1, replica_groups=mesh['dp'=2,'tensor'=8,'line'=2,'column'=8] {'line','dp','column'}, dimensions={0} | all-to-all | bytes 2097152 | tf_op jit(solution)/shard_map/cond/branch_0_fun/all_to_all | solution.py:335
  48.1 0.0 copy-done.8
  48.1 0.0 copy-done.10
  48.1 0.0 copy-done.12
  48.1 4.3 %convolve.2 = f32[32,96,128]{2,1,0:T(8,128)S(1)} custom-call(f32[32,16,128]{2,1,0:T(8,128)S(1)} %all-to-all-done.refs_0_, f32[32,64,128]{2,1,0:T(8,128)S(1)} %all_to_all.20.refs_1_, bf16[256,256]{1,0:T(8,128)(2,1)S(1)} %copy-done.12, bf16[256,256]{1,0:T(8,128)(2,1)S(1)} %copy-done.10, f32[17,2,8,128]{3,2,1,0:T(8,128)S(1)} %copy-done.8), custom_call_target="tpu_custom_call" | custom-call | tf_op jit(solution)/shard_map/cond/branch_0_fun/convolve/pallas_call | solution.py:288
  52.5 0.0 copy-start
  52.5 0.0 copy-start.2
  52.5 0.0 copy-start.4
  52.5 0.0 copy-start.6
  52.5 0.0 copy-start.14
  52.5 36.3 %all_to_all.21.refs_0_ = f32[32,96,128]{2,1,0:T(8,128)S(1)} all-to-all(f32[32,96,128]{2,1,0:T(8,128)S(1)} %convolve.2), channel_id=1, replica_groups=mesh['dp'=2,'tensor'=8,'line'=2,'column'=8] {'line','dp','column'}, dimensions={0} | all-to-all | bytes 3145728 | tf_op jit(solution)/shard_map/cond/branch_0_fun/all_to_all | solution.py:335
  88.8 0.0 copy-done
  88.8 0.0 copy-done.2
  88.8 0.0 copy-done.4
  88.8 0.0 copy-done.6
  88.8 0.0 copy-done.14
  88.8 1.5 %unpack.2 = (bf16[128,1024]{1,0:T(8,128)(2,1)}, bf16[128,1024]{1,0:T(8,128)(2,1)}, bf16[128,1024]{1,0:T(8,128)(2,1)}, f32[128,1024]{1,0:T(8,128)}) custom-call(f32[32,96,128]{2,1,0:T(8,128)S(1)} %all_to_all.21.refs_0_, bf16[128,1024]{1,0:T(8,128)(2,1)S(1)} %copy-done, bf16[128,1024]{1,0:T(8,128)(2,1)S(1)} %copy-done.2, f32[1,1024]{1,0:T(1,128)S(1)} %bitcast.2, ...), custom_call_target="tpu_custom_call" | custom-call | tf_op jit(solution)/shard_map/cond/branch_0_fun/unpack/pallas_call | solution.py:306
Async XLA Ops:
  2.4 22.1 %all-to-all-start = ((f32[32,16,128]{2,1,0:T(8,128)}), f32[32,16,128]{2,1,0:T(8,128)S(1)}, u32[]{:S(2)}, u32[]{:S(2)}) async-start(f32[32,16,128]{2,1,0:T(8,128)} %pack.3), calls=%async_computation | async-start | bytes 524288 | tf_op jit(solution)/shard_map/cond/branch_0_fun/all_to_all | solution.py:335
  15.9 32.3 %copy-start.8 = (f32[17,2,8,128]{3,2,1,0:T(8,128)S(1)}, f32[17,2,8,128]{3,2,1,0:T(8,128)}, u32[]{:S(2)}) copy-start(f32[17,2,8,128]{3,2,1,0:T(8,128)} %get-tuple-element.43.refs_4_) | copy-start | bytes 417796 | tf_op jit(solution)/shard_map/cond
  15.9 32.3 %copy-start.10 = (bf16[256,256]{1,0:T(8,128)(2,1)S(1)}, bf16[256,256]{1,0:T(8,128)(2,1)}, u32[]{:S(2)}) copy-start(bf16[256,256]{1,0:T(8,128)(2,1)} %get-tuple-element.42.refs_3_) | copy-start | bytes 393220 | tf_op jit(solution)/shard_map/cond
  15.9 32.2 %copy-start.12 = (bf16[256,256]{1,0:T(8,128)(2,1)S(1)}, bf16[256,256]{1,0:T(8,128)(2,1)}, u32[]{:S(2)}) copy-start(bf16[256,256]{1,0:T(8,128)(2,1)} %get-tuple-element.41.refs_2_) | copy-start | bytes 393220 | tf_op jit(solution)/shard_map/cond
  52.5 36.4 %copy-start = (bf16[128,1024]{1,0:T(8,128)(2,1)S(1)}, bf16[128,1024]{1,0:T(8,128)(2,1)}, u32[]{:S(2)}) copy-start(bf16[128,1024]{1,0:T(8,128)(2,1)} %get-tuple-element.37.refs_0_.refs_1_) | copy-start | bytes 786436 | tf_op jit(solution)/shard_map/cond
  52.5 36.3 %copy-start.2 = (bf16[128,1024]{1,0:T(8,128)(2,1)S(1)}, bf16[128,1024]{1,0:T(8,128)(2,1)}, u32[]{:S(2)}) copy-start(bf16[128,1024]{1,0:T(8,128)(2,1)} %get-tuple-element.38.refs_1_.refs_2_) | copy-start | bytes 786436 | tf_op jit(solution)/shard_map/cond
  52.5 36.3 %copy-start.4 = (bf16[128,1024]{1,0:T(8,128)(2,1)S(1)}, bf16[128,1024]{1,0:T(8,128)(2,1)}, u32[]{:S(2)}) copy-start(bf16[128,1024]{1,0:T(8,128)(2,1)} %get-tuple-element.39.refs_2_.refs_4_) | copy-start | bytes 786436 | tf_op jit(solution)/shard_map/cond
  52.5 36.3 %copy-start.6 = (bf16[128,1024]{1,0:T(8,128)(2,1)S(1)}, bf16[128,1024]{1,0:T(8,128)(2,1)}, u32[]{:S(2)}) copy-start(bf16[128,1024]{1,0:T(8,128)(2,1)} %get-tuple-element.40.refs_3_.refs_5_) | copy-start | bytes 786436 | tf_op jit(solution)/shard_map/cond
  52.5 36.3 %copy-start.14 = (f32[1024]{0:T(1024)S(1)}, f32[1024]{0:T(1024)}, u32[]{:S(2)}) copy-start(f32[1024]{0:T(1024)} %get-tuple-element.44) | copy-start | bytes 12292 | tf_op jit(solution)/shard_map/cond

commit v8 on v7

--- a/solution.py
+++ b/solution.py
@@ -317,7 +317,7 @@
 
 GROUP = 3
 PACK_WIDTH = 512
-UNPACK_WIDTH = 512
+UNPACK_WIDTH = 1024
 MIXED, FILTER, GRAD = 0, 1, 2
 FACTORS = (2, 1, 2)
 WHOLE = ((MIXED, FILTER, GRAD),)

time: 90.6 us -> 90.6 us (level)
  no operation moved by 1% of the time
where the time goes in v8:
time: 90.6 us; the launch traced here: 90.4 us
  blocking collectives  59.9 us (66%)
  starting transfers between devices  11.9 us (13%)
  Pallas kernels  9.16 us (10%)
  waiting for transfers between devices  8.64 us (10%)
    all_to_all x2, blocking collectives, exchange(): lax.all_to_all(operand, AXES, split_axis=0, concat_axis=0, tiled=True)  59.9 us
    all_to_all x1, starting transfers between devices, exchange(): lax.all_to_all(operand, AXES, split_axis=0, concat_axis=0, tiled=True)  11.9 us
    all_to_all x1, waiting for transfers between devices, exchange(): lax.all_to_all(operand, AXES, split_axis=0, concat_axis=0, tiled=True)  8.64 us
    pallas_call x1, Pallas kernels, convolve(): pl.pallas_call(lambda *refs: convolve_kernel(shape, plan, *refs), out_sha...  4.32 us
    pallas_call x2, Pallas kernels, pack(): pl.pallas_call(lambda *refs: pack_kernel(share, parts, members, *refs), g...  3.34 us
  transfers between devices with their start and end apart: 1, of which 1 were waited for; matrix products, arithmetic and copies ran while one was open for 0% of the time, Pallas kernels for 2%

profile of v8, /device:TPU:1, one launch (start us, length us, event | category | flops | bytes accessed | tf_op | source)
XLA Modules:
  0.0 90.4 jit_solution(98720085382263353)
XLA Ops:
  0.6 89.7 %conditional.1 = ((bf16[128,1024]{1,0:T(8,128)(2,1)}, bf16[128,1024]{1,0:T(8,128)(2,1)}, bf16[128,1024]{1,0:T(8,128)(2,1)}, f32[128,1024]{1,0:T(8,128)})) conditional(s32[]{:T(128)} %convert_element_type.3, (bf16[128,1024]{1,0:T(8,128)(2,1)}, bf16[128,1024]{1,0:T(8,128)(2,1)}, bf16[128,1024]{1,0:T(8,128)(2,1)}, bf16[128,1024]{1,0:T(8,128)(2,1)}, ...), branch_computations={%region_0.1_spmd, %region_1.2_spmd} | conditional | bytes 11845896 | solution.py:350
  0.7 1.8 %pack.3 = f32[32,16,128]{2,1,0:T(8,128)} custom-call(bf16[128,1024]{1,0:T(8,128)(2,1)} %get-tuple-element.36.refs_0_), custom_call_target="tpu_custom_call" | custom-call | tf_op jit(solution)/shard_map/cond/branch_0_fun/pack/pallas_call | solution.py:272
  2.4 11.9 %all-to-all-start = ((f32[32,16,128]{2,1,0:T(8,128)}), f32[32,16,128]{2,1,0:T(8,128)S(1)}, u32[]{:S(2)}, u32[]{:S(2)}) async-start(f32[32,16,128]{2,1,0:T(8,128)} %pack.3), calls=%async_computation | async-start | bytes 524288 | tf_op jit(solution)/shard_map/cond/branch_0_fun/all_to_all | solution.py:335
  14.3 1.5 %pack.4 = f32[32,64,128]{2,1,0:T(8,128)S(1)} custom-call(bf16[128,1024]{1,0:T(8,128)(2,1)} %get-tuple-element.37.refs_0_.refs_1_, bf16[128,1024]{1,0:T(8,128)(2,1)} %get-tuple-element.38.refs_1_.refs_2_, bf16[128,1024]{1,0:T(8,128)(2,1)} %get-tuple-element.39.refs_2_.refs_4_, bf16[128,1024]{1,0:T(8,128)(2,1)} %get-tuple-element.40.refs_3_.refs_5_), custom_call_target="tpu_custom_call" | custom-call | tf_op jit(solution)/shard_map/cond/branch_0_fun/pack/pallas_call | solution.py:272
  15.9 0.0 copy-start.8
  15.9 0.0 copy-start.10
  15.9 0.0 copy-start.12
  15.9 8.6 %all-to-all-done.refs_0_ = f32[32,16,128]{2,1,0:T(8,128)S(1)} async-done(((f32[32,16,128]{2,1,0:T(8,128)}), f32[32,16,128]{2,1,0:T(8,128)S(1)}, u32[]{:S(2)}, u32[]{:S(2)}) %all-to-all-start) | async-done | bytes 262176 | tf_op jit(solution)/shard_map/cond/branch_0_fun/all_to_all | solution.py:335
  24.5 23.6 %all_to_all.20.refs_1_ = f32[32,64,128]{2,1,0:T(8,128)S(1)} all-to-all(f32[32,64,128]{2,1,0:T(8,128)S(1)} %pack.4), channel_id=1, replica_groups=mesh['dp'=2,'tensor'=8,'line'=2,'column'=8] {'line','dp','column'}, dimensions={0} | all-to-all | bytes 2097152 | tf_op jit(solution)/shard_map/cond/branch_0_fun/all_to_all | solution.py:335
  48.1 0.0 copy-done.8
  48.1 0.0 copy-done.10
  48.1 0.0 copy-done.12
  48.1 4.3 %convolve.2 = f32[32,96,128]{2,1,0:T(8,128)S(1)} custom-call(f32[32,16,128]{2,1,0:T(8,128)S(1)} %all-to-all-done.refs_0_, f32[32,64,128]{2,1,0:T(8,128)S(1)} %all_to_all.20.refs_1_, bf16[256,256]{1,0:T(8,128)(2,1)S(1)} %copy-done.12, bf16[256,256]{1,0:T(8,128)(2,1)S(1)} %copy-done.10, f32[17,2,8,128]{3,2,1,0:T(8,128)S(1)} %copy-done.8), custom_call_target="tpu_custom_call" | custom-call | tf_op jit(solution)/shard_map/cond/branch_0_fun/convolve/pallas_call | solution.py:288
  52.5 0.0 copy-start
  52.5 0.0 copy-start.2
  52.5 0.0 copy-start.4
  52.5 0.0 copy-start.6
  52.5 0.0 copy-start.14
  52.5 36.3 %all_to_all.21.refs_0_ = f32[32,96,128]{2,1,0:T(8,128)S(1)} all-to-all(f32[32,96,128]{2,1,0:T(8,128)S(1)} %convolve.2), channel_id=1, replica_groups=mesh['dp'=2,'tensor'=8,'line'=2,'column'=8] {'line','dp','column'}, dimensions={0} | all-to-all | bytes 3145728 | tf_op jit(solution)/shard_map/cond/branch_0_fun/all_to_all | solution.py:335
  88.8 0.0 copy-done
  88.8 0.0 copy-done.2
  88.8 0.0 copy-done.4
  88.8 0.0 copy-done.6
  88.8 0.0 copy-done.14
  88.8 1.5 %unpack.2 = (bf16[128,1024]{1,0:T(8,128)(2,1)}, bf16[128,1024]{1,0:T(8,128)(2,1)}, bf16[128,1024]{1,0:T(8,128)(2,1)}, f32[128,1024]{1,0:T(8,128)}) custom-call(f32[32,96,128]{2,1,0:T(8,128)S(1)} %all_to_all.21.refs_0_, bf16[128,1024]{1,0:T(8,128)(2,1)S(1)} %copy-done, bf16[128,1024]{1,0:T(8,128)(2,1)S(1)} %copy-done.2, f32[1,1024]{1,0:T(1,128)S(1)} %bitcast.2, ...), custom_call_target="tpu_custom_call" | custom-call | tf_op jit(solution)/shard_map/cond/branch_0_fun/unpack/pallas_call | solution.py:306
Async XLA Ops:
  2.4 22.1 %all-to-all-start = ((f32[32,16,128]{2,1,0:T(8,128)}), f32[32,16,128]{2,1,0:T(8,128)S(1)}, u32[]{:S(2)}, u32[]{:S(2)}) async-start(f32[32,16,128]{2,1,0:T(8,128)} %pack.3), calls=%async_computation | async-start | bytes 524288 | tf_op jit(solution)/shard_map/cond/branch_0_fun/all_to_all | solution.py:335
  15.9 32.3 %copy-start.8 = (f32[17,2,8,128]{3,2,1,0:T(8,128)S(1)}, f32[17,2,8,128]{3,2,1,0:T(8,128)}, u32[]{:S(2)}) copy-start(f32[17,2,8,128]{3,2,1,0:T(8,128)} %get-tuple-element.43.refs_4_) | copy-start | bytes 417796 | tf_op jit(solution)/shard_map/cond
  15.9 32.3 %copy-start.10 = (bf16[256,256]{1,0:T(8,128)(2,1)S(1)}, bf16[256,256]{1,0:T(8,128)(2,1)}, u32[]{:S(2)}) copy-start(bf16[256,256]{1,0:T(8,128)(2,1)} %get-tuple-element.42.refs_3_) | copy-start | bytes 393220 | tf_op jit(solution)/shard_map/cond
  15.9 32.2 %copy-start.12 = (bf16[256,256]{1,0:T(8,128)(2,1)S(1)}, bf16[256,256]{1,0:T(8,128)(2,1)}, u32[]{:S(2)}) copy-start(bf16[256,256]{1,0:T(8,128)(2,1)} %get-tuple-element.41.refs_2_) | copy-start | bytes 393220 | tf_op jit(solution)/shard_map/cond
  52.5 36.4 %copy-start = (bf16[128,1024]{1,0:T(8,128)(2,1)S(1)}, bf16[128,1024]{1,0:T(8,128)(2,1)}, u32[]{:S(2)}) copy-start(bf16[128,1024]{1,0:T(8,128)(2,1)} %get-tuple-element.37.refs_0_.refs_1_) | copy-start | bytes 786436 | tf_op jit(solution)/shard_map/cond
  52.5 36.3 %copy-start.2 = (bf16[128,1024]{1,0:T(8,128)(2,1)S(1)}, bf16[128,1024]{1,0:T(8,128)(2,1)}, u32[]{:S(2)}) copy-start(bf16[128,1024]{1,0:T(8,128)(2,1)} %get-tuple-element.38.refs_1_.refs_2_) | copy-start | bytes 786436 | tf_op jit(solution)/shard_map/cond
  52.5 36.3 %copy-start.4 = (bf16[128,1024]{1,0:T(8,128)(2,1)S(1)}, bf16[128,1024]{1,0:T(8,128)(2,1)}, u32[]{:S(2)}) copy-start(bf16[128,1024]{1,0:T(8,128)(2,1)} %get-tuple-element.39.refs_2_.refs_4_) | copy-start | bytes 786436 | tf_op jit(solution)/shard_map/cond
  52.5 36.3 %copy-start.6 = (bf16[128,1024]{1,0:T(8,128)(2,1)S(1)}, bf16[128,1024]{1,0:T(8,128)(2,1)}, u32[]{:S(2)}) copy-start(bf16[128,1024]{1,0:T(8,128)(2,1)} %get-tuple-element.40.refs_3_.refs_5_) | copy-start | bytes 786436 | tf_op jit(solution)/shard_map/cond
  52.5 36.3 %copy-start.14 = (f32[1024]{0:T(1024)S(1)}, f32[1024]{0:T(1024)}, u32[]{:S(2)}) copy-start(f32[1024]{0:T(1024)} %get-tuple-element.44) | copy-start | bytes 12292 | tf_op jit(solution)/shard_map/cond
